TPU v7x, 256 devices: a whole 4x4x8 slice. The times are simulated.
256 devices in a mesh: seq: 32 (over y, z), kvh: 8 (over x, core).
Axes of the slice: x: 4, y: 4, z: 8, core: 2. Of those that a mesh axis runs over, the one named last changes fastest.
Arguments:
- queries: bfloat16 [512, 8192], P(('seq', 'kvh')), may hold values from -47 to 47
- keys: bfloat16 [32768, 1024], P(('seq', 'kvh')), may hold values from -6 to 6
- omega: bfloat16 [32768, 4096], P('seq', 'kvh'), may hold values from -6 to 6
- block_offsets: int32 [4], replicated, may hold values from 0 to 255, as said below
Outputs:
- basis_out: float32 [512, 4096], P('seq', 'kvh')
- projection: float32 [4096, 32768], P('kvh', 'seq')
Inputs may be any that keep to these rules, and one draw needn't show every extreme that they name: `block_offsets`: block i lies in [i * s, (i + 1) * s) with s = 64; the first block is 0 and the last is 255.
All inputs are finite; a program needn't handle non-finite values.
Results may differ from a plain program's by a relative error of at most 0.012.
The roundings to bfloat16 on the way count: a program that leaves them out, or rounds other values in their place, can miss the bound.
Values may be sent and summed in bfloat16 or wider, within the bound.
A program may use at most 64 MiB of HBM per device.

v0:
```python
import math

import jax
import jax.numpy as jnp
from jax import lax
from jax.sharding import PartitionSpec as P

POWER = 2
QBLK = 128


very_negative = -1e30


def combined_all(value, axis, join):
    pieces = jax.tree.map(lambda part: lax.all_gather(part, axis), value)
    head = jax.tree.map(lambda part: part[0], pieces)
    tail = jax.tree.map(lambda part: part[1:], pieces)
    so_far, _ = lax.scan(lambda so_far, share: (join(so_far, share), None), head, tail)
    return so_far


def gram_matrix(sketch):
    return jnp.einsum(
        "ngr,ngs->grs",
        sketch,
        sketch,
        precision=lax.Precision.HIGHEST,
        preferred_element_type=jnp.float32,
    )


def apply_factor(sketch, gram_total):
    factor = jnp.linalg.cholesky(gram_total)
    solved = jax.scipy.linalg.solve_triangular(factor, jnp.transpose(sketch, (1, 2, 0)), lower=True)
    return jnp.transpose(solved, (2, 0, 1))


def merge_softmax(first_pair, second_pair):
    largest = jnp.maximum(first_pair[0], second_pair[0])
    total_sum = first_pair[1] * jnp.exp(first_pair[0] - largest) + second_pair[1] * jnp.exp(
        second_pair[0] - largest
    )
    return (largest, total_sum)


def unchanged(value):
    return value


def body(queries, keys, omega, block_offsets):
    seq_count = lax.axis_size("seq")
    seq_rank = lax.axis_index("seq")
    local_queries, local_keys = (
        lax.all_to_all(queries, "kvh", split_axis=1, concat_axis=0, tiled=True),
        lax.all_to_all(keys, "kvh", split_axis=1, concat_axis=0, tiled=True),
    )
    slab_rows = lax.all_gather(local_queries, "seq", axis=0, tiled=True)
    head_size = local_keys.shape[1]
    groups = local_queries.shape[1] // head_size
    sketch_width = omega.shape[1] // groups
    key_count = local_keys.shape[0]
    half_keys = key_count // 2
    query_total = slab_rows.shape[0]
    own_count = local_queries.shape[0]
    block_count = query_total // QBLK
    tile_count = 2 * block_count
    inverse_root = 1.0 / math.sqrt(head_size)
    query_blocks = slab_rows.reshape(block_count, QBLK, groups, head_size)
    key_halves = local_keys.reshape(2, half_keys, head_size)
    omega_halves = omega.reshape(2, half_keys, groups, sketch_width)
    first_start = seq_rank * key_count
    second_start = seq_rank * key_count + half_keys
    half_starts = jnp.stack([first_start, second_start])

    def is_active(block_index, half_index):
        offset = lax.dynamic_index_in_dim(block_offsets, block_index, 0, keepdims=False)
        key_start = lax.dynamic_index_in_dim(half_starts, half_index, 0, keepdims=False)
        return offset * QBLK + QBLK - 1 >= key_start

    def tile_scores(block_index, half_index):
        query_rows = lax.dynamic_index_in_dim(query_blocks, block_index, 0, keepdims=False)
        key_rows = lax.dynamic_index_in_dim(key_halves, half_index, 0, keepdims=False)
        scores = (
            jnp.einsum("qgd,kd->gqk", query_rows, key_rows, preferred_element_type=jnp.float32)
            * inverse_root
        )
        offset = lax.dynamic_index_in_dim(block_offsets, block_index, 0, keepdims=False)
        key_start = lax.dynamic_index_in_dim(half_starts, half_index, 0, keepdims=False)
        query_pos = offset * QBLK + jnp.arange(QBLK, dtype=jnp.int32)
        key_pos = key_start + jnp.arange(half_keys, dtype=jnp.int32)
        allowed = key_pos[None, :] <= query_pos[:, None]
        return (scores, allowed)

    def stats_tile(tile_index, running):
        block_index = tile_index // 2
        half_index = tile_index % 2

        def stats_update(running):
            maxima, totals = running
            scores, allowed = tile_scores(block_index, half_index)
            masked = jnp.where(allowed[None], scores, very_negative)
            row_start = block_index * QBLK
            old_max = lax.dynamic_slice_in_dim(maxima, row_start, QBLK, 1)
            old_total = lax.dynamic_slice_in_dim(totals, row_start, QBLK, 1)
            new_max = jnp.maximum(old_max, jnp.max(masked, axis=-1))
            weights = jnp.where(allowed[None], jnp.exp(scores - new_max[..., None]), 0.0)
            new_total = old_total * jnp.exp(old_max - new_max) + jnp.sum(weights, axis=-1)
            maxima = lax.dynamic_update_slice_in_dim(maxima, new_max, row_start, 1)
            totals = lax.dynamic_update_slice_in_dim(totals, new_total, row_start, 1)
            return (maxima, totals)

        return lax.cond(is_active(block_index, half_index), stats_update, unchanged, running)

    start_max = jnp.full((groups, query_total), very_negative, jnp.float32)
    start_total = jnp.zeros((groups, query_total), jnp.float32)
    maxima, totals = lax.fori_loop(0, tile_count, stats_tile, (start_max, start_total))
    maxima, totals = combined_all((maxima, totals), "seq", merge_softmax)

    def tile_weights(block_index, half_index):
        scores, allowed = tile_scores(block_index, half_index)
        row_start = block_index * QBLK
        largest = lax.dynamic_slice_in_dim(maxima, row_start, QBLK, 1)
        total_rows = lax.dynamic_slice_in_dim(totals, row_start, QBLK, 1)
        weights = jnp.where(
            allowed[None], jnp.exp(scores - largest[..., None]) / total_rows[..., None], 0.0
        )
        return weights.astype(jnp.bfloat16)

    def forward(sketch_keys):

        def forward_tile(tile_index, result):
            block_index = tile_index // 2
            half_index = tile_index % 2

            def forward_update(result):
                weights = tile_weights(block_index, half_index)
                columns = lax.dynamic_index_in_dim(sketch_keys, half_index, 0, keepdims=False)
                product = jnp.einsum(
                    "gqk,kgr->qgr", weights, columns, preferred_element_type=jnp.float32
                )
                row_start = block_index * QBLK
                previous = lax.dynamic_slice_in_dim(result, row_start, QBLK, 0)
                return lax.dynamic_update_slice_in_dim(result, previous + product, row_start, 0)

            return lax.cond(is_active(block_index, half_index), forward_update, unchanged, result)

        initial = jnp.zeros((query_total, groups, sketch_width), jnp.float32)
        return lax.fori_loop(0, tile_count, forward_tile, initial)

    def backward(slab_basis):

        def backward_tile(tile_index, result):
            block_index = tile_index // 2
            half_index = tile_index % 2

            def backward_update(result):
                weights = tile_weights(block_index, half_index)
                row_start = block_index * QBLK
                query_side = lax.dynamic_slice_in_dim(slab_basis, row_start, QBLK, 0)
                product = jnp.einsum(
                    "gqk,qgr->kgr", weights, query_side, preferred_element_type=jnp.float32
                )
                previous = lax.dynamic_index_in_dim(result, half_index, 0, keepdims=False)
                return lax.dynamic_update_index_in_dim(result, previous + product, half_index, 0)

            return lax.cond(is_active(block_index, half_index), backward_update, unchanged, result)

        initial = jnp.zeros((2, half_keys, groups, sketch_width), jnp.float32)
        return lax.fori_loop(0, tile_count, backward_tile, initial)

    def range_basis(partial_value):
        flattened = partial_value.reshape(query_total, groups * sketch_width)
        owned = lax.psum_scatter(flattened, "seq", scatter_dimension=0, tiled=True).reshape(
            own_count, groups, sketch_width
        )
        gram_total = lax.psum(gram_matrix(owned), "seq")
        owned_basis = apply_factor(owned, gram_total)
        rounded = owned_basis.astype(jnp.bfloat16).reshape(own_count, groups * sketch_width)
        slab_basis = lax.all_gather(rounded, "seq", axis=0, tiled=True).reshape(
            query_total, groups, sketch_width
        )
        return (owned_basis, slab_basis)

    owned_basis, slab_basis = range_basis(forward(omega_halves))
    for power_step in range(POWER):
        key_side = backward(slab_basis).astype(jnp.bfloat16)
        owned_basis, slab_basis = range_basis(forward(key_side))
    projected = backward(slab_basis)
    key_total = key_count * seq_count
    projection = jnp.transpose(
        projected.reshape(key_count, groups, sketch_width), (1, 2, 0)
    ).reshape(groups * sketch_width, key_count) * math.sqrt(key_total)
    basis_out = owned_basis.reshape(own_count, groups * sketch_width) * math.sqrt(query_total)
    return (basis_out, projection)


def solution(mesh):
    placed = (P(("seq", "kvh"), None), P(("seq", "kvh"), None), P("seq", "kvh"), P())
    return jax.shard_map(
        body,
        mesh=mesh,
        in_specs=placed,
        out_specs=(P("seq", "kvh"), P("kvh", "seq")),
        check_vma=False,
    )
```

profile of v0, /device:TPU:24, one launch (start us, length us, event | category | flops | bytes accessed | tf_op | source)
XLA Modules:
  0.0 2040.6 jit_solution(2189012349922750271)
XLA Ops:
  7.2 9.9 all_to_all.35
  18.5 4.0 all-to-all-start
  22.6 2.8 reshape.432
  25.4 2.2 copy.146
  27.8 66.2 %all-gather.4.cloned.1.call-done = bf16[512,1024]{1,0:T(8,128)(2,1)} async-done(((bf16[16,1024]{1,0:T(8,128)(2,1)}), bf16[512,1024]{1,0:T(8,128)(2,1)}) %all-gather.4.cloned.1.call-update) | async-done | bytes 1048592 | tf_op jit(solution)/shard_map/all_gather | solution.py:58
  94.0 1.5 copy.198
  96.7 31.8 %while.158 = (s32[]{:T(128)}, f32[8,512]{1,0:T(8,128)S(1)}, f32[8,512]{1,0:T(8,128)S(1)}, s32[4]{0:T(128)S(1)}, s32[2]{0:T(128)S(1)}, /*index=5*/bf16[2,512,128]...) while((s32[]{:T(128)}, f32[8,512]{1,0:T(8,128)S(1)}, ...), condition=%wide.region_5.6_spmd, body=%wide.region_0.5_spmd.sunk | while | flops 137956000 | bytes 4904592 | solution.py:117
  116.0 4.9 conditional.14
  118.9 1.5 fusion
  123.6 4.9 conditional.14
  126.5 1.5 fusion
  128.5 72.1 %all-gather = f32[256,512]{1,0:T(8,128)S(1)} all-gather(f32[8,512]{1,0:T(8,128)S(1)} %get-tuple-element.2522), channel_id=2, replica_groups=mesh['seq'=32,'kvh'=8] {'seq'}, dimensions={0}, use_global_device_ids=true | all-gather | bytes 540672 | tf_op jit(solution)/shard_map/all_gather | solution.py:16
  200.7 46.3 %all-gather.1 = f32[256,512]{1,0:T(8,128)S(1)} all-gather(f32[8,512]{1,0:T(8,128)S(1)} %get-tuple-element.2523), channel_id=3, replica_groups=mesh['seq'=32,'kvh'=8] {'seq'}, dimensions={0}, use_global_device_ids=true | all-gather | bytes 540672 | tf_op jit(solution)/shard_map/all_gather | solution.py:16
  247.1 1.4 while.159
  248.7 31.5 %while.160 = (s32[]{:T(128)}, f32[512,8,64]{0,2,1:T(8,128)S(1)}, s32[4]{0:T(128)S(1)}, s32[2]{0:T(128)S(1)}, bf16[2,512,8,64]{1,3,2,0:T(8,128)(2,1)S(1)}, /*inde...) while((s32[]{:T(128)}, f32[512,8,64]{0,2,1:T(8,128)S(1)}, ...), condition=%wide.region_11.12_spmd, body=%wide.region_8.11_spmd.sunk | while | flops 204079776 | bytes 1605252 | solution.py:149
  267.9 4.8 conditional.15
  270.9 1.8 fusion.19
  275.4 4.8 conditional.15
  278.4 1.8 fusion.19
  280.2 1.3 copy.148
  281.6 233.7 %reduce-scatter.4.cloned.1.call-done = f32[16,512]{1,0:T(8,128)} async-done(((f32[512,512]{1,0:T(8,128)}), f32[16,512]{1,0:T(8,128)}) %reduce-scatter.4.cloned.1.call-update) | async-done | bytes 32784 | tf_op jit(solution)/shard_map/reduce_scatter | solution.py:174
  516.2 1.3 fusion.190
  517.6 143.1 %all-reduce.4.cloned.1.call-done = f32[8,64,64]{1,2,0:T(8,128)} async-done(((f32[8,64,64]{1,2,0:T(8,128)}), f32[8,64,64]{1,2,0:T(8,128)}) %all-reduce.4.cloned.1.call-update) | async-done | bytes 131088 | tf_op jit(solution)/shard_map/psum | solution.py:177
  662.8 46.9 %custom-call.10 = f32[8,64,64]{2,1,0:T(8,128)S(1)} custom-call(f32[8,64,64]{2,1,0:T(8,128)S(1)} %fusion.182), custom_call_target="Cholesky" | custom-call | tf_op jit(solution)/shard_map/jit(cholesky)/cholesky | solution.py:34
  709.9 39.3 %custom-call.11 = f32[8,1,64,64]{2,3,1,0:T(8,128)S(1)} custom-call(f32[8,1,64,64]{3,2,1,0:T(8,128)S(1)} %select_bitcast_fusion.2), custom_call_target="InvertDiagBlocksLowerTriangular" | custom-call | tf_op jit(solution)/shard_map/jit(_solve_triangular)/vmap()/triangular_solve | solution.py:35
  749.7 48.4 %all_gather.29 = bf16[512,512]{1,0:T(8,128)(2,1)S(1)} all-gather(bf16[16,512]{1,0:T(8,128)(2,1)S(1)} %reshape.400), channel_id=1, replica_groups=mesh['seq'=32,'kvh'=8] {'seq'}, dimensions={0}, use_global_device_ids=true | all-gather | bytes 540672 | tf_op jit(solution)/shard_map/all_gather | solution.py:180
  799.4 30.8 %while.161 = (s32[]{:T(128)}, f32[2,512,8,64]{1,3,2,0:T(8,128)S(1)}, s32[4]{0:T(128)S(1)}, s32[2]{0:T(128)S(1)}, bf16[512,8,64]{0,2,1:T(8,128)(2,1)}, /*index=5*...) while((s32[]{:T(128)}, f32[2,512,8,64]{1,3,2,0:T(8,128)S(1)}, ...), condition=%wide.region_19.22_spmd, body=%wide.region_16.21_spmd.sunk | while | flops 204276384 | bytes 4882056 | solution.py:170
  817.8 4.9 conditional.16
  820.7 2.0 fusion.47
  825.3 4.9 conditional.16
  828.3 2.0 fusion.47
  830.5 28.3 %while.162 = (s32[]{:T(128)}, f32[512,8,64]{0,2,1:T(8,128)S(1)}, s32[4]{0:T(128)S(1)}, s32[2]{0:T(128)S(1)}, bf16[2,512,8,64]{1,3,2,0:T(8,128)(2,1)S(1)}, /*inde...) while((s32[]{:T(128)}, f32[512,8,64]{0,2,1:T(8,128)S(1)}, ...), condition=%wide.region_23.26_spmd, body=%wide.region_20.25_spmd.sunk | while | flops 204079776 | bytes 1605252 | solution.py:149
  847.4 4.5 conditional.17
  850.1 1.8 fusion.73
  854.3 4.5 conditional.17
  857.0 1.8 fusion.73
  858.8 1.3 copy.159
  860.2 255.6 %reduce-scatter.6.cloned.1.call-done = f32[16,512]{1,0:T(8,128)} async-done(((f32[512,512]{1,0:T(8,128)}), f32[16,512]{1,0:T(8,128)}) %reduce-scatter.6.cloned.1.call-update) | async-done | bytes 32784 | tf_op jit(solution)/shard_map/reduce_scatter | solution.py:174
  1118.1 142.9 %all-reduce.6.cloned.1.call-done = f32[8,64,64]{1,2,0:T(8,128)} async-done(((f32[8,64,64]{1,2,0:T(8,128)}), f32[8,64,64]{1,2,0:T(8,128)}) %all-reduce.6.cloned.1.call-update) | async-done | bytes 131088 | tf_op jit(solution)/shard_map/psum | solution.py:177
  1263.1 46.9 %custom-call.12 = f32[8,64,64]{2,1,0:T(8,128)S(1)} custom-call(f32[8,64,64]{2,1,0:T(8,128)S(1)} %fusion.180), custom_call_target="Cholesky" | custom-call | tf_op jit(solution)/shard_map/jit(cholesky)/cholesky | solution.py:34
  1310.3 39.3 %custom-call.13 = f32[8,1,64,64]{2,3,1,0:T(8,128)S(1)} custom-call(f32[8,1,64,64]{3,2,1,0:T(8,128)S(1)} %select_bitcast_fusion.1), custom_call_target="InvertDiagBlocksLowerTriangular" | custom-call | tf_op jit(solution)/shard_map/jit(_solve_triangular)/vmap()/triangular_solve | solution.py:35
  1350.1 48.2 %all_gather.30 = bf16[512,512]{1,0:T(8,128)(2,1)S(1)} all-gather(bf16[16,512]{1,0:T(8,128)(2,1)S(1)} %reshape.404), channel_id=1, replica_groups=mesh['seq'=32,'kvh'=8] {'seq'}, dimensions={0}, use_global_device_ids=true | all-gather | bytes 540672 | tf_op jit(solution)/shard_map/all_gather | solution.py:180
  1399.6 30.8 %while.163 = (s32[]{:T(128)}, f32[2,512,8,64]{1,3,2,0:T(8,128)S(1)}, s32[4]{0:T(128)S(1)}, s32[2]{0:T(128)S(1)}, bf16[512,8,64]{0,2,1:T(8,128)(2,1)}, /*index=5*...) while((s32[]{:T(128)}, f32[2,512,8,64]{1,3,2,0:T(8,128)S(1)}, ...), condition=%wide.region_29.32_spmd, body=%wide.region_26.31_spmd.sunk | while | flops 204276384 | bytes 4882056 | solution.py:170
  1417.9 4.9 conditional.18
  1420.9 2.0 fusion.101
  1425.5 4.9 conditional.18
  1428.4 2.0 fusion.101
  1430.7 28.3 %while.164 = (s32[]{:T(128)}, f32[512,8,64]{0,2,1:T(8,128)S(1)}, s32[4]{0:T(128)S(1)}, s32[2]{0:T(128)S(1)}, bf16[2,512,8,64]{1,3,2,0:T(8,128)(2,1)S(1)}, /*inde...) while((s32[]{:T(128)}, f32[512,8,64]{0,2,1:T(8,128)S(1)}, ...), condition=%wide.region_33.36_spmd, body=%wide.region_30.35_spmd.sunk | while | flops 204079776 | bytes 1605252 | solution.py:149
  1447.5 4.5 conditional.19
  1450.2 1.8 fusion.127
  1454.4 4.5 conditional.19
  1457.1 1.8 fusion.127
  1459.0 1.3 copy.170
  1460.6 255.4 %reduce-scatter.8.cloned.1.call-done = f32[16,512]{1,0:T(8,128)} async-done(((f32[512,512]{1,0:T(8,128)}), f32[16,512]{1,0:T(8,128)}) %reduce-scatter.8.cloned.1.call-update) | async-done | bytes 32784 | tf_op jit(solution)/shard_map/reduce_scatter | solution.py:174
  1718.2 143.2 %all-reduce.8.cloned.1.call-done = f32[8,64,64]{1,2,0:T(8,128)} async-done(((f32[8,64,64]{1,2,0:T(8,128)}), f32[8,64,64]{1,2,0:T(8,128)}) %all-reduce.8.cloned.1.call-update) | async-done | bytes 131088 | tf_op jit(solution)/shard_map/psum | solution.py:177
  1863.4 46.9 %custom-call.14 = f32[8,64,64]{2,1,0:T(8,128)S(1)} custom-call(f32[8,64,64]{2,1,0:T(8,128)S(1)} %fusion.178), custom_call_target="Cholesky" | custom-call | tf_op jit(solution)/shard_map/jit(cholesky)/cholesky | solution.py:34
  1910.6 39.3 %custom-call.15 = f32[8,1,64,64]{2,3,1,0:T(8,128)S(1)} custom-call(f32[8,1,64,64]{3,2,1,0:T(8,128)S(1)} %select_bitcast_fusion), custom_call_target="InvertDiagBlocksLowerTriangular" | custom-call | tf_op jit(solution)/shard_map/jit(_solve_triangular)/vmap()/triangular_solve | solution.py:35
  1951.1 48.2 %all_gather.31 = bf16[512,512]{1,0:T(8,128)(2,1)S(1)} all-gather(bf16[16,512]{1,0:T(8,128)(2,1)S(1)} %reshape.408), channel_id=1, replica_groups=mesh['seq'=32,'kvh'=8] {'seq'}, dimensions={0}, use_global_device_ids=true | all-gather | bytes 540672 | tf_op jit(solution)/shard_map/all_gather | solution.py:180
  2000.6 30.6 %while.165 = (s32[]{:T(128)}, f32[2,512,8,64]{1,3,2,0:T(8,128)S(1)}, s32[4]{0:T(128)S(1)}, s32[2]{0:T(128)S(1)}, bf16[512,8,64]{0,2,1:T(8,128)(2,1)}, /*index=5*...) while((s32[]{:T(128)}, f32[2,512,8,64]{1,3,2,0:T(8,128)S(1)}, ...), condition=%wide.region_39.42_spmd, body=%wide.region_36.41_spmd.sunk | while | flops 204276384 | bytes 4882056 | solution.py:170
  2018.9 4.8 conditional.20
  2021.8 2.0 fusion.155
  2026.4 4.8 conditional.20
  2029.2 2.0 fusion.155
  2031.5 1.5 copy.197
  (361 shorter events, 125.8 us)
Async XLA Ops:
  7.2 10.6 copy-start
  7.2 86.8 %all-gather.4.cloned.1.call-start = ((), (), s32[]{:S(2)}) async-start(), calls=%async_computation.5 | async-start | bytes 1081344 | tf_op jit(solution)/shard_map/all_gather | solution.py:58
  18.5 78.1 %all-to-all-start = ((bf16[128,8,128]{2,0,1:T(8,128)(2,1)}), bf16[128,8,128]{2,0,1:T(8,128)(2,1)}, u32[]{:S(2)}, u32[]{:S(2)}) async-start(bf16[128,8,128]{2,0,1:T(8,128)(2,1)} %copy_bitcast_fusion), calls=%async_computation | async-start | bytes 524288 | tf_op jit(solution)/shard_map/all_to_all | solution.py:56
  22.6 492.7 %reduce-scatter.4.cloned.1.call-start = ((), (), s32[]{:S(2)}) async-start(), calls=%async_computation.6 | async-start | bytes 1081344 | tf_op jit(solution)/shard_map/reduce_scatter | solution.py:174
  94.0 2.7 copy-start.3
  200.7 48.0 %copy-start.1 = (bf16[2,512,8,64]{1,3,2,0:T(8,128)(2,1)S(1)}, bf16[2,512,8,64]{1,3,2,0:T(8,128)(2,1)}, u32[]{:S(2)}) copy-start(bf16[2,512,8,64]{1,3,2,0:T(8,128)(2,1)} %copy.146) | copy-start | bytes 3145732
  281.6 379.1 %all-reduce.4.cloned.1.call-start = ((), (), s32[]{:S(2)}) async-start(), calls=%async_computation.7 | async-start | bytes 524288 | tf_op jit(solution)/shard_map/psum | solution.py:177
  517.5 598.4 %reduce-scatter.6.cloned.1.call-start = ((), (), s32[]{:S(2)}) async-start(), calls=%async_computation.8 | async-start | bytes 1081344 | tf_op jit(solution)/shard_map/reduce_scatter | solution.py:174
  860.2 400.9 %all-reduce.6.cloned.1.call-start = ((), (), s32[]{:S(2)}) async-start(), calls=%async_computation.9 | async-start | bytes 524288 | tf_op jit(solution)/shard_map/psum | solution.py:177
  1118.0 598.0 %reduce-scatter.8.cloned.1.call-start = ((), (), s32[]{:S(2)}) async-start(), calls=%async_computation.10 | async-start | bytes 1081344 | tf_op jit(solution)/shard_map/reduce_scatter | solution.py:174
  1460.3 401.1 %all-reduce.8.cloned.1.call-start = ((), (), s32[]{:S(2)}) async-start(), calls=%async_computation.11 | async-start | bytes 524288 | tf_op jit(solution)/shard_map/psum | solution.py:177
  2031.5 1.5 copy-start.2
Sparse Core Ops, SparseCore 0:
  17.9 76.0 all-gather.3
  281.7 233.5 reduce-scatter.3
  518.8 141.8 all-reduce.3
  860.3 255.5 reduce-scatter.5
  1119.2 141.8 all-reduce.5
  1460.4 255.5 reduce-scatter.7
  1719.5 141.8 all-reduce.7
where the time goes:
time: 2070 us; the launch traced here: 2040 us
  waiting for transfers between devices  1240 us (60%)
  other arithmetic  276 us (13%)
  blocking collectives  273 us (13%)
  local copies, waits for them, and re-layouts  115 us (6%)
  loops' own time  85.2 us (4%)
  matrix products  31.6 us (2%)
    reduce_scatter x3, waiting for transfers between devices, range_basis(): lax.psum_scatter(flattened, 'seq', scatter_dimension=0, tiled=True)  745 us
    psum x3, waiting for transfers between devices, range_basis(): gram_total = lax.psum(gram_matrix(owned), 'seq')  429 us
    all_gather x3, blocking collectives, range_basis(): lax.all_gather(rounded, 'seq', axis=0, tiled=True)  145 us
    another operation x10, other arithmetic, apply_factor(): factor = jnp.linalg.cholesky(gram_total)  141 us
    all_gather x2, blocking collectives, combined_all(): pieces = jax.tree.map(lambda part: lax.all_gather(part, axis), value)  118 us
    another operation x7, other arithmetic, apply_factor(): jax.scipy.linalg.solve_triangular(factor, jnp.transpose(sketch, (1, 2, 0)...  118 us
    all_gather x1, waiting for transfers between devices, body(): slab_rows = lax.all_gather(local_queries, 'seq', axis=0, tiled=True)  66.2 us
  transfers between devices with their start and end apart: 8, of which 7 were waited for; matrix products, arithmetic and copies ran while one was open for 0% of the time, Pallas kernels for 0%

commit v1 on v0

v1 whole, which is shorter than its diff:
```python
import functools
import math

import jax
import jax.numpy as jnp
from jax import lax
from jax.experimental import pallas as pl
from jax.experimental.pallas import tpu as pltpu
from jax.sharding import PartitionSpec as P

MESH = pl.DeviceIdType.MESH
F32 = jnp.float32
BF16 = jnp.bfloat16
HIGHEST = lax.Precision.HIGHEST

SEQ = 32
KVH = 8
PLANES = 4
RING = 8
HEADS = 8
HEAD = 128
RANK = 64
BLOCK = 128
QUERIES = 512
WIDE = QUERIES - BLOCK
KEYS = 1024
POWER = 2
CHUNK = 128

MASKED = -1e30
LOWEST = -1e29
SCALE = math.log2(math.e) / math.sqrt(HEAD)

LANES = (((1,), (1,)), ((), ()))
PLAIN = (((1,), (0,)), ((), ()))


def dot(left, right, dims=PLAIN, precision=None):
    return lax.dot_general(left, right, dims, precision=precision, preferred_element_type=F32)


def each(count, step, start=0):
    def run(index, carry):
        step(index)
        return carry

    lax.fori_loop(start, count, run, 0)


def inverse_factor(gram):
    lanes = lax.broadcasted_iota(jnp.int32, (RANK, RANK), 1)
    rows = lax.broadcasted_iota(jnp.int32, (RANK, RANK), 0)
    start = jnp.concatenate([gram, jnp.where(lanes == rows, 1.0, 0.0)], axis=1)
    sub = lax.broadcasted_iota(jnp.int32, (8, 2 * RANK), 0)

    def spread(tile, lane):
        return jnp.broadcast_to(tile[:, lane : lane + 1], tile.shape)

    def lift(tile, row):
        return jnp.broadcast_to(tile[row : row + 1, :], tile.shape)

    def block(step, tiles):
        pivot = tiles[0]
        columns = [spread(pivot, j) for j in range(8)]
        inverses, upper, roots = [], [], jnp.zeros_like(pivot)
        for j in range(8):
            diagonal = lift(columns[j], j)
            inverse = 1.0 / diagonal
            inverses.append(inverse)
            roots = jnp.where(sub == j, lax.rsqrt(diagonal), roots)
            factor = jnp.where(sub > j, columns[j] * inverse, 0.0)
            pivot = pivot - factor * lift(pivot, j)
            across = {}
            for other in range(j + 1, 8):
                across[other] = lift(columns[other], j)
                columns[other] = columns[other] - factor * across[other]
            upper.append(across)
        pivot_rows = [lift(pivot, j) for j in range(8)]
        later = []
        for index in range(1, 8):
            tile = tiles[index]
            live = jnp.where(step + index < 8, 1.0, 0.0)
            columns = [spread(tile, j) * live for j in range(8)]
            for j in range(8):
                factor = columns[j] * inverses[j]
                tile = tile - factor * pivot_rows[j]
                for other in range(j + 1, 8):
                    columns[other] = columns[other] - factor * upper[j][other]
            later.append(tile)
        later.append(pivot * roots)
        return tuple(pltpu.roll(tile, 2 * RANK - 8, 1) for tile in later)

    tiles = lax.fori_loop(0, 8, block, tuple(start[8 * i : 8 * i + 8] for i in range(8)))
    return jnp.concatenate(tiles, axis=0)[:, :RANK]


def orthonormal_rows(panel):
    gram = dot(panel, panel, LANES, HIGHEST)
    return dot(inverse_factor(gram), panel, PLAIN, HIGHEST)


def kernel(
    offsets,
    q_ref,
    k_hbm,
    omega_hbm,
    basis_ref,
    proj_hbm,
    q_wide,
    q_tiles,
    q_got,
    q_flat,
    q_turned,
    q_own,
    q_all,
    k_all,
    omega_rows,
    omega_turned,
    scores,
    scores_first,
    probs,
    probs_first,
    stat_out,
    stat_in,
    stat_all,
    part_wide,
    part_wide_in,
    part,
    part_in,
    basis,
    staged,
    local_sem,
    store_sem,
    qk_send,
    qk_recv,
    kk_send,
    kk_recv,
    qs_send,
    qs_recv,
    st_send,
    st_recv,
    pw_send,
    pw_recv,
    sa_send,
    sa_recv,
    pt_send,
    pt_recv,
    bs_send,
    bs_recv,
):
    s = lax.axis_index("seq")
    k = lax.axis_index("kvh")
    y = lax.div(s, RING)
    z = lax.rem(s, RING)
    core = lax.rem(k, 2)

    def owner_of(head):
        return lax.rem(head + core, 2) * RING + head

    owns = owner_of(z) == s

    def to_kvh(src, dst, send, recv, target):
        return pltpu.make_async_remote_copy(
            src_ref=src, dst_ref=dst, send_sem=send, recv_sem=recv,
            device_id={"kvh": target}, device_id_type=MESH,
        )

    def to_seq(src, dst, send, recv, target):
        return pltpu.make_async_remote_copy(
            src_ref=src, dst_ref=dst, send_sem=send, recv_sem=recv,
            device_id={"seq": target}, device_id_type=MESH,
        )

    barrier = pltpu.get_barrier_semaphore()

    def greet_seq(d):
        @pl.when(d != s)
        def _():
            pl.semaphore_signal(barrier, inc=1, device_id={"seq": d}, device_id_type=MESH)

    def greet_kvh(d):
        @pl.when(d != k)
        def _():
            pl.semaphore_signal(barrier, inc=1, device_id={"kvh": d}, device_id_type=MESH)

    each(KVH, greet_kvh)
    each(SEQ, greet_seq)

    omega_copy = pltpu.make_async_copy(omega_hbm, omega_rows, local_sem.at[0])
    omega_copy.start()
    keys_copy = pltpu.make_async_copy(
        k_hbm.at[:, pl.ds(pl.multiple_of(k * HEAD, HEAD), HEAD)], k_all.at[k], local_sem.at[1]
    )
    keys_copy.start()

    q_now = q_ref[...].astype(F32)
    for tile in range(KVH * HEADS):
        q_wide[2 * tile : 2 * tile + 2, :] = q_now[:, tile * HEAD : (tile + 1) * HEAD]
    q_tiles[...] = q_wide[...].astype(BF16).reshape(KVH, 16, HEAD)
    q_got[k] = q_tiles[k]

    def clear_queries(d):
        q_all[:, d] = jnp.zeros((HEADS, 16, HEAD), BF16)

    each(RING * y, clear_queries)
    basis[...] = jnp.zeros(basis.shape, BF16)

    pl.semaphore_wait(barrier, SEQ - 1 + KVH - 1)

    def q_copy(d, slot):
        return to_kvh(q_tiles.at[d], q_got.at[slot], qk_send.at[d], qk_recv.at[slot], d)

    def k_copy(d, slot):
        columns = pl.ds(pl.multiple_of(d * HEAD, HEAD), HEAD)
        return to_kvh(k_hbm.at[:, columns], k_all.at[slot], kk_send.at[d], kk_recv.at[slot], d)

    def others_kvh(step):
        def run(d):
            @pl.when(d != k)
            def _():
                step(d)

        each(KVH, run)

    others_kvh(lambda d: q_copy(d, k).start())
    others_kvh(lambda d: k_copy(d, k).start())
    others_kvh(lambda d: q_copy(d, d).wait_recv())

    q_flat[...] = q_got[...].astype(F32).reshape(KVH * 16, HEAD)
    for pair in range(16):
        q_turned[8 * pair : 8 * pair + 8, :] = q_flat[pl.ds(pair, 8, stride=16), :]
    q_own[...] = q_turned[...].astype(BF16).reshape(HEADS, 16, HEAD)
    q_all[:, s] = q_own[...]

    def q_spread(d, slot):
        return to_seq(q_own, q_all.at[:, slot], qs_send.at[d], qs_recv.at[slot], d)

    def others_seq(step, start=0, stop=SEQ):
        def run(d):
            @pl.when(d != s)
            def _():
                step(d)

        each(stop, run, start)

    others_seq(lambda d: q_spread(d, s).start(), 0, RING * (y + 1))

    omega_copy.wait()
    for tile in range(4):
        turned = omega_rows[:, tile * 128 : (tile + 1) * 128].astype(F32).T.astype(BF16)
        omega_turned[2 * tile] = turned[:RANK]
        omega_turned[2 * tile + 1] = turned[RANK:]

    keys_copy.wait()
    others_kvh(lambda d: k_copy(d, d).wait_recv())
    others_seq(lambda d: q_spread(d, d).wait_recv(), RING * y, SEQ)

    def positions(block, count):
        lane = lax.broadcasted_iota(jnp.int32, (1, count), 1)
        inside = lax.rem(lane, BLOCK)
        place = lax.rem(inside, 16)
        row = inside - place + 2 * lax.rem(place, 8) + lax.div(place, 8)
        which = lax.div(lane, BLOCK) + block
        first = jnp.zeros((1, count), jnp.int32)
        for index in range(4):
            first = jnp.where(which == index, offsets[index], first)
        return first * BLOCK + row - s * KEYS

    limit = positions(1, WIDE)
    limit_first = positions(0, BLOCK)
    key_row = lax.broadcasted_iota(jnp.int32, (CHUNK, 1), 0)

    def fold(tile, join):
        pieces = tile.reshape(CHUNK // 8, 8, tile.shape[1])
        return join(pieces, axis=0)

    def send_part(source, landing, send, recv, head, start):
        target = owner_of(head)
        for plane in range(PLANES):
            @pl.when((y == plane) & (target != s))
            def _():
                blocks = pl.ds(plane, PLANES - plane)
                copy = to_seq(
                    source.at[head, blocks], landing.at[s, blocks], send.at[head], recv.at[s], target
                )
                if start:
                    copy.start()
                else:
                    copy.wait_send()

    def stat_copy(head):
        target = owner_of(head)
        return to_seq(stat_out.at[head], stat_in.at[s], st_send.at[head], st_recv.at[s], target)

    def first_head(index):
        head = lax.rem(index + z, HEADS)
        q_head = q_all[head, 8:32].reshape(WIDE, HEAD)
        largest = jnp.full((8, WIDE), LOWEST, F32)
        for chunk in range(KEYS // CHUNK):
            piece = dot(k_all[chunk], q_head, LANES)
            piece = jnp.where(key_row + chunk * CHUNK <= limit, piece, MASKED)
            scores[head, chunk * CHUNK : (chunk + 1) * CHUNK, :] = piece
            largest = jnp.maximum(largest, fold(piece, jnp.max))
        top = jnp.max(largest, axis=0, keepdims=True)
        total = jnp.zeros((8, WIDE), F32)
        for chunk in range(KEYS // CHUNK):
            at = slice(chunk * CHUNK, (chunk + 1) * CHUNK)
            weight = jnp.exp2((scores[head, at, :] - top) * SCALE)
            total = total + fold(weight, jnp.sum)
            probs[head, at, :] = weight.astype(BF16)
        q_first = q_all[head, 0:8].reshape(BLOCK, HEAD)
        piece = jnp.where(key_row <= limit_first, dot(k_all[0], q_first, LANES), MASKED)
        scores_first[head] = piece
        top_first = jnp.maximum(jnp.max(piece, axis=0, keepdims=True), LOWEST)
        weight = jnp.exp2((piece - top_first) * SCALE)
        probs_first[head] = weight.astype(BF16)
        stat_out[head, 0:1, :] = jnp.concatenate([top_first, top], axis=1)
        stat_out[head, 1:2, :] = jnp.concatenate(
            [jnp.sum(weight, axis=0, keepdims=True), jnp.sum(total, axis=0, keepdims=True)], axis=1
        )
        forward(head, omega_turned[head], part_wide, part_wide_in)

        @pl.when(owner_of(head) == s)
        def _():
            stat_in[s] = stat_out[head]

        @pl.when(owner_of(head) != s)
        def _():
            stat_copy(head).start()

        send_part(part_wide, part_wide_in, pw_send, pw_recv, head, True)

    def forward(head, panel, out, landing):
        product = dot(panel, probs[head])
        first = dot(panel[:, :BLOCK], probs_first[head])
        pieces = [first] + [product[:, b * BLOCK : (b + 1) * BLOCK] for b in range(3)]
        for index, piece in enumerate(pieces):
            out[head, index] = piece.astype(out.dtype)

        @pl.when(owner_of(head) == s)
        def _():
            for index, piece in enumerate(pieces):
                landing[s, index] = piece.astype(out.dtype)

    def backward(head):
        low = jnp.concatenate([basis[head, 1], basis[head, 2], basis[head, 3]], axis=1)
        product = dot(low, probs[head], LANES)
        first = dot(basis[head, 0], probs_first[head], LANES)
        return jnp.concatenate([product[:, :BLOCK] + first, product[:, BLOCK:]], axis=1)

    each(HEADS, first_head)

    def wait_parts(source, landing, send, recv):
        for plane in range(PLANES):
            blocks = pl.ds(plane, PLANES - plane)

            def run(d, blocks=blocks):
                to_seq(
                    source.at[0, blocks], landing.at[d, blocks], send.at[0], recv.at[d], d
                ).wait_recv()

            others_seq(run, plane * RING, plane * RING + RING)

    def stat_share(d):
        return to_seq(stat_all.at[z], stat_all.at[z], sa_send.at[d], sa_recv.at[z], d)

    def basis_share(plane, d, head):
        blocks = pl.ds(plane, PLANES - plane)
        return to_seq(basis.at[head, blocks], basis.at[head, blocks], bs_send.at[d], bs_recv.at[head], d)

    def share_basis(start):
        for plane in range(PLANES):
            def run(d, plane=plane):
                copy = basis_share(plane, d, z)
                if start:
                    copy.start()
                else:
                    copy.wait_send()

            others_seq(run, plane * RING, plane * RING + RING)

    def store_basis(rows):
        for block in range(PLANES):
            basis[z, block] = rows[:, block * BLOCK : (block + 1) * BLOCK].astype(BF16)

    def add_parts(landing, weigh):
        totals = tuple(jnp.zeros((RANK, BLOCK), F32) for _ in range(PLANES))
        for plane in range(PLANES):
            def run(index, totals, plane=plane):
                d = plane * RING + index
                weight = weigh(d)
                return totals[:plane] + tuple(
                    totals[b] + (
                        landing[d, b].astype(F32)
                        if weight is None
                        else landing[d, b] * weight[:, b * BLOCK : (b + 1) * BLOCK]
                    )
                    for b in range(plane, PLANES)
                )

            totals = lax.fori_loop(0, RING, run, totals)
        return jnp.concatenate(totals, axis=1)

    @pl.when(owns)
    def _():
        others_seq(lambda d: to_seq(stat_out.at[0], stat_in.at[d], st_send.at[0], st_recv.at[d], d).wait_recv())
        top = lax.fori_loop(
            0, SEQ, lambda d, so_far: jnp.maximum(so_far, stat_in[d, 0:1, :]),
            jnp.full((1, QUERIES), MASKED, F32),
        )
        total = lax.fori_loop(
            0, SEQ,
            lambda d, so_far: so_far
            + stat_in[d, 1:2, :] * jnp.exp2((stat_in[d, 0:1, :] - top) * SCALE),
            jnp.zeros((1, QUERIES), F32),
        )
        inverse = 1.0 / total
        stat_all[z, 0:1, :] = top
        stat_all[z, 1:2, :] = inverse
        others_seq(lambda d: stat_share(d).start())
        wait_parts(part_wide, part_wide_in, pw_send, pw_recv)
        panel = add_parts(
            part_wide_in, lambda d: jnp.exp2((stat_in[d, 0:1, :] - top) * SCALE)
        ) * inverse
        store_basis(orthonormal_rows(panel))
        share_basis(True)

    def normalise(index):
        head = lax.rem(index + z, HEADS)

        @pl.when(owner_of(head) != s)
        def _():
            to_seq(
                stat_all.at[head], stat_all.at[head], sa_send.at[0], sa_recv.at[head], owner_of(head)
            ).wait_recv()

        top = stat_all[head, 0:1, :]
        inverse = stat_all[head, 1:2, :]
        for chunk in range(KEYS // CHUNK):
            at = slice(chunk * CHUNK, (chunk + 1) * CHUNK)
            weight = jnp.exp2((scores[head, at, :] - top[:, BLOCK:]) * SCALE)
            probs[head, at, :] = (weight * inverse[:, BLOCK:]).astype(BF16)
        weight = jnp.exp2((scores_first[head] - top[:, :BLOCK]) * SCALE)
        probs_first[head] = (weight * inverse[:, :BLOCK]).astype(BF16)

    each(HEADS, normalise)

    def wait_basis(head):
        target = owner_of(head)
        for plane in range(PLANES):
            @pl.when((y == plane) & (target != s))
            def _():
                basis_share(plane, target, head).wait_recv()

    def power_step(step):
        def one_head(index):
            head = lax.rem(index + z, HEADS)
            wait_basis(head)
            forward(head, backward(head).astype(BF16), part, part_in)
            send_part(part, part_in, pt_send, pt_recv, head, True)

        each(HEADS, one_head)

        @pl.when(owns)
        def _():
            wait_parts(part, part_in, pt_send, pt_recv)
            rows = orthonormal_rows(add_parts(part_in, lambda d: None))
            share_basis(False)
            store_basis(rows)
            share_basis(True)

        each(HEADS, lambda head: send_part(part, part_in, pt_send, pt_recv, head, False))

    each(POWER, power_step)

    def store_copy(head):
        rows = pl.ds(pl.multiple_of(head * RANK, RANK), RANK)
        return pltpu.make_async_copy(staged.at[rows], proj_hbm.at[rows], store_sem.at[head])

    def last_head(index):
        head = lax.rem(index + z, HEADS)
        wait_basis(head)
        rows = pl.ds(pl.multiple_of(head * RANK, RANK), RANK)
        staged[rows, :] = backward(head) * math.sqrt(SEQ * KEYS)
        store_copy(head).start()

    each(HEADS, last_head)

    row = lax.broadcasted_iota(jnp.int32, (16, QUERIES), 0)
    lane = lax.broadcasted_iota(jnp.int32, (16, QUERIES), 1)
    chosen = lane == s * 16 + 8 * lax.rem(row, 2) + lax.div(row, 2)
    chosen = jnp.where(chosen, 1.0, 0.0).astype(BF16)
    total = jnp.zeros((16, HEADS * RANK), F32)
    for block in range(PLANES):
        total = total + dot(
            chosen[:, block * BLOCK : (block + 1) * BLOCK],
            basis[:, block].reshape(HEADS * RANK, BLOCK),
            LANES,
        )
    basis_ref[...] = total * math.sqrt(QUERIES)

    each(HEADS, lambda head: store_copy(head).wait())
    others_kvh(lambda d: q_copy(d, k).wait_send())
    others_kvh(lambda d: k_copy(d, k).wait_send())
    others_seq(lambda d: q_spread(d, s).wait_send(), 0, RING * (y + 1))

    def sent(head):
        @pl.when(owner_of(head) != s)
        def _():
            stat_copy(head).wait_send()

        send_part(part_wide, part_wide_in, pw_send, pw_recv, head, False)

    each(HEADS, sent)

    @pl.when(owns)
    def _():
        others_seq(lambda d: stat_share(d).wait_send())
        share_basis(False)


def body(queries, keys, omega, block_offsets):
    vmem = lambda shape, kind: pltpu.VMEM(shape, kind)
    dma = lambda *shape: pltpu.SemaphoreType.DMA(shape)
    return pl.pallas_call(
        kernel,
        out_shape=(
            jax.ShapeDtypeStruct((16, HEADS * RANK), F32),
            jax.ShapeDtypeStruct((HEADS * RANK, KEYS), F32),
        ),
        in_specs=[
            pl.BlockSpec(memory_space=pltpu.SMEM),
            pl.BlockSpec(memory_space=pltpu.VMEM),
            pl.BlockSpec(memory_space=pl.ANY),
            pl.BlockSpec(memory_space=pl.ANY),
        ],
        out_specs=(
            pl.BlockSpec(memory_space=pltpu.VMEM),
            pl.BlockSpec(memory_space=pl.ANY),
        ),
        scratch_shapes=[
            vmem((128, HEAD), F32),
            vmem((KVH, 16, HEAD), BF16),
            vmem((KVH, 16, HEAD), BF16),
            vmem((128, HEAD), F32),
            vmem((128, HEAD), F32),
            vmem((HEADS, 16, HEAD), BF16),
            vmem((HEADS, SEQ, 16, HEAD), BF16),
            vmem((KVH, 128, HEAD), BF16),
            vmem((KEYS, HEADS * RANK), BF16),
            vmem((HEADS, RANK, KEYS), BF16),
            vmem((HEADS, KEYS, WIDE), F32),
            vmem((HEADS, BLOCK, BLOCK), F32),
            vmem((HEADS, KEYS, WIDE), BF16),
            vmem((HEADS, BLOCK, BLOCK), BF16),
            vmem((HEADS, 2, QUERIES), F32),
            vmem((SEQ, 2, QUERIES), F32),
            vmem((HEADS, 2, QUERIES), F32),
            vmem((HEADS, PLANES, RANK, BLOCK), F32),
            vmem((SEQ, PLANES, RANK, BLOCK), F32),
            vmem((HEADS, PLANES, RANK, BLOCK), BF16),
            vmem((SEQ, PLANES, RANK, BLOCK), BF16),
            vmem((HEADS, PLANES, RANK, BLOCK), BF16),
            vmem((HEADS * RANK, KEYS), F32),
            dma(2),
            dma(HEADS),
            dma(KVH), dma(KVH),
            dma(KVH), dma(KVH),
            dma(SEQ), dma(SEQ),
            dma(HEADS), dma(SEQ),
            dma(HEADS), dma(SEQ),
            dma(SEQ), dma(HEADS),
            dma(HEADS), dma(SEQ),
            dma(SEQ), dma(HEADS),
        ],
        compiler_params=pltpu.CompilerParams(
            collective_id=0, has_side_effects=True, vmem_limit_bytes=56 * 2**20
        ),
        cost_estimate=pl.CostEstimate(
            flops=6 * 10**9, bytes_accessed=8 * 2**20, transcendentals=8 * 10**6
        ),
        name="range_finder",
    )(block_offsets, queries, keys, omega)


def solution(mesh):
    placed = (P(("seq", "kvh"), None), P(("seq", "kvh"), None), P("seq", "kvh"), P())
    return jax.shard_map(
        body,
        mesh=mesh,
        in_specs=placed,
        out_specs=(P("seq", "kvh"), P("kvh", "seq")),
        check_vma=False,
    )
```

time: 2070 us -> 160 us (0.08); the launches traced: 2040 us -> 159 us
  waiting for transfers between devices: 1240 us -> 0 us
  other arithmetic: 276 us -> 0 us
  blocking collectives: 273 us -> 0 us
  Pallas kernels: 0 us -> 154 us
  local copies, waits for them, and re-layouts: 115 us -> 4.53 us
  loops' own time: 85.2 us -> 0 us
  matrix products: 31.6 us -> 0 us
    reduce_scatter x3 -> x0, waiting for transfers between devices: 745 us -> none  [range_basis(): lax.psum_scatter(flattened, 'seq', scatter_dimension=0, tiled=True)]
    psum x3 -> x0, waiting for transfers between devices: 429 us -> none  [range_basis(): gram_total = lax.psum(gram_matrix(owned), 'seq')]
    all_gather x5 -> x0, blocking collectives: 263 us -> none  [the longest x3 145 us: range_basis(): lax.all_gather(rounded, 'seq', axis=0, tiled=True)]
    another operation x18 -> x0, other arithmetic: 260 us -> none  [the longest x10 141 us: apply_factor(): factor = jnp.linalg.cholesky(gram_total)]
    pallas_call x0 -> x1, Pallas kernels: none -> 154 us  [body(): pl.pallas_call(kernel, out_shape=(jax.ShapeDtypeStruct((16, HEADS * RANK)...]
    dynamic_slice x158 -> x0, local copies, waits for them, and re-layouts: 89.6 us -> none  [the longest x56 35.6 us: is_active(): lax.dynamic_index_in_dim(block_offsets, block_index, 0, keepdims=False)]
    another operation x64 -> x0, loops' own time: 85.2 us -> none  [the longest x3 31.8 us: backward(): return lax.fori_loop(0, tile_count, backward_tile, initial)]
    all_gather x1 -> x0, waiting for transfers between devices: 66.2 us -> none  [body(): slab_rows = lax.all_gather(local_queries, 'seq', axis=0, tiled=True)]
  transfers between devices with their start and end apart: 8 -> 0, of which waited for: 7 -> 0; matrix products, arithmetic and copies ran while one was open for 0% -> 0% of each run, Pallas kernels for 0% -> 0%
where the time goes in v1:
time: 160 us; the launch traced here: 159 us
  Pallas kernels  154 us (96%)
  local copies, waits for them, and re-layouts  4.53 us (3%)
    pallas_call x1, Pallas kernels, body(): pl.pallas_call(kernel, out_shape=(jax.ShapeDtypeStruct((16, HEADS * RANK)...  154 us
    unnamed x2, local copies, waits for them, and re-layouts  4.53 us

profile of v1, /device:TPU:24, one launch (start us, length us, event | category | flops | bytes accessed | tf_op | source)
XLA Modules:
  0.0 159.5 jit_solution(14781731953403113117)
XLA Ops:
  0.6 154.3 %range_finder.1 = (f32[16,512]{1,0:T(8,128)}, f32[512,1024]{1,0:T(8,128)}) custom-call(s32[4]{0:T(128)} %offsets.1, bf16[2,8192]{1,0:T(2,128)(2,1)} %q_ref.1, bf16[128,1024]{1,0:T(8,128)(2,1)} %k_hbm.1, bf16[1024,512]{1,0:T(8,128)(2,1)} %omega_hbm.1), custom_call_target="tpu_custom_call" | custom-call | flops 6000000000 | bytes 8388608 | tf_op jit(solution)/shard_map/range_finder/pallas_call | solution.py:525
  155.0 1.4 copy.8
  156.3 3.2 %copy.9 = f32[512,1024]{1,0:T(8,128)} copy(f32[512,1024]{1,0:T(8,128)} %get-tuple-element.5) | data formatting | bytes 4194304

commit v2 on v1

v2 whole, which is shorter than its diff:
```python
import functools
import math

import jax
import jax.numpy as jnp
from jax import lax
from jax.experimental import pallas as pl
from jax.experimental.pallas import tpu as pltpu
from jax.sharding import PartitionSpec as P

MESH = pl.DeviceIdType.MESH
F32 = jnp.float32
BF16 = jnp.bfloat16
HIGHEST = lax.Precision.HIGHEST

SEQ = 32
KVH = 8
PLANES = 4
RING = 8
HEADS = 8
HEAD = 128
RANK = 64
BLOCK = 128
QUERIES = 512
WIDE = QUERIES - BLOCK
KEYS = 1024
POWER = 2
CHUNK = 128

MASKED = -1e30
LOWEST = -1e29
SCALE = math.log2(math.e) / math.sqrt(HEAD)

LANES = (((1,), (1,)), ((), ()))
PLAIN = (((1,), (0,)), ((), ()))


def dot(left, right, dims=PLAIN, precision=None):
    return lax.dot_general(left, right, dims, precision=precision, preferred_element_type=F32)


def each(count, step, start=0):
    def run(index, carry):
        step(index)
        return carry

    lax.fori_loop(start, count, run, 0)


def inverse_factor(gram):
    lanes = lax.broadcasted_iota(jnp.int32, (RANK, RANK), 1)
    rows = lax.broadcasted_iota(jnp.int32, (RANK, RANK), 0)
    start = jnp.concatenate([gram, jnp.where(lanes == rows, 1.0, 0.0)], axis=1)
    sub = lax.broadcasted_iota(jnp.int32, (8, 2 * RANK), 0)

    def spread(tile, lane):
        return jnp.broadcast_to(tile[:, lane : lane + 1], tile.shape)

    def lift(tile, row):
        return jnp.broadcast_to(tile[row : row + 1, :], tile.shape)

    def block(step, tiles):
        pivot = tiles[0]
        columns = [spread(pivot, j) for j in range(8)]
        inverses, upper, roots = [], [], jnp.zeros_like(pivot)
        for j in range(8):
            diagonal = lift(columns[j], j)
            inverse = 1.0 / diagonal
            inverses.append(inverse)
            roots = jnp.where(sub == j, lax.rsqrt(diagonal), roots)
            factor = jnp.where(sub > j, columns[j] * inverse, 0.0)
            pivot = pivot - factor * lift(pivot, j)
            across = {}
            for other in range(j + 1, 8):
                across[other] = lift(columns[other], j)
                columns[other] = columns[other] - factor * across[other]
            upper.append(across)
        pivot_rows = [lift(pivot, j) for j in range(8)]
        later = []
        for index in range(1, 8):
            tile = tiles[index]
            live = jnp.where(step + index < 8, 1.0, 0.0)
            columns = [spread(tile, j) * live for j in range(8)]
            for j in range(8):
                factor = columns[j] * inverses[j]
                tile = tile - factor * pivot_rows[j]
                for other in range(j + 1, 8):
                    columns[other] = columns[other] - factor * upper[j][other]
            later.append(tile)
        later.append(pivot * roots)
        return tuple(pltpu.roll(tile, 2 * RANK - 8, 1) for tile in later)

    tiles = lax.fori_loop(0, 8, block, tuple(start[8 * i : 8 * i + 8] for i in range(8)))
    return jnp.concatenate(tiles, axis=0)[:, :RANK]


def orthonormal_rows(panel):
    gram = dot(panel, panel, LANES, HIGHEST)
    return dot(inverse_factor(gram), panel, PLAIN, HIGHEST)


def kernel(
    offsets,
    q_ref,
    k_hbm,
    omega_hbm,
    basis_ref,
    proj_hbm,
    q_wide,
    q_tiles,
    q_got,
    q_flat,
    q_turned,
    q_own,
    q_all,
    k_all,
    omega_rows,
    omega_turned,
    scores,
    scores_first,
    probs,
    probs_first,
    stat_out,
    stat_y,
    stat_sum,
    stat_z,
    stat_all,
    wide_out,
    wide_y,
    wide_sum,
    wide_z,
    part_out,
    part_y,
    part_sum,
    part_z,
    basis,
    staged,
    local_sem,
    store_sem,
    qk_send,
    qk_recv,
    kk_send,
    kk_recv,
    qz_send,
    qf_send,
    q_recv,
    sty_send,
    sty_recv,
    stz_send,
    stz_recv,
    sta_send,
    stb_send,
    st_recv,
    wy_send,
    wy_recv,
    wz_send,
    wz_recv,
    py_send,
    py_recv,
    pz_send,
    pz_recv,
    bz_send,
    by_send,
    b_recv,
):
    s = lax.axis_index("seq")
    k = lax.axis_index("kvh")
    y = lax.div(s, RING)
    z = lax.rem(s, RING)
    core = lax.rem(k, 2)

    def owner_z(j):
        return 2 * (2 * j + core)

    own_j = lax.div(z, 4)
    own_head = 2 * y + own_j
    owns = owner_z(own_j) == z

    def at_seq(plane, place):
        return plane * RING + place

    def remote(src, dst, send, recv, **target):
        return pltpu.make_async_remote_copy(
            src_ref=src, dst_ref=dst, send_sem=send, recv_sem=recv,
            device_id=target, device_id_type=MESH,
        )

    def others(count, me, step):
        def run(d):
            @pl.when(d != me)
            def _():
                step(d)

        each(count, run)

    barrier = pltpu.get_barrier_semaphore()

    def greet(**target):
        pl.semaphore_signal(barrier, inc=1, device_id=target, device_id_type=MESH)

    others(KVH, k, lambda d: greet(kvh=d))
    others(RING, z, lambda d: greet(seq=at_seq(y, d)))
    others(PLANES, y, lambda d: greet(seq=at_seq(d, z)))

    omega_copy = pltpu.make_async_copy(omega_hbm, omega_rows, local_sem.at[0])
    omega_copy.start()
    keys_copy = pltpu.make_async_copy(
        k_hbm.at[:, pl.ds(pl.multiple_of(k * HEAD, HEAD), HEAD)], k_all.at[k], local_sem.at[1]
    )
    keys_copy.start()

    q_now = q_ref[...].astype(F32)
    for tile in range(KVH * HEADS):
        q_wide[2 * tile : 2 * tile + 2, :] = q_now[:, tile * HEAD : (tile + 1) * HEAD]
    q_tiles[...] = q_wide[...].astype(BF16).reshape(KVH, 16, HEAD)
    q_got[k] = q_tiles[k]

    basis[...] = jnp.zeros(basis.shape, BF16)
    probs_first[...] = jnp.zeros(probs_first.shape, BF16)
    stat_out[:, 0:1, :] = jnp.full((HEADS, 1, QUERIES), LOWEST, F32)
    stat_out[:, 1:2, :] = jnp.zeros((HEADS, 1, QUERIES), F32)

    @pl.when(y >= 2)
    def _():
        def clear(head):
            probs[head] = jnp.zeros((KEYS, WIDE), BF16)

        each(HEADS, clear)

    pl.semaphore_wait(barrier, KVH - 1 + RING - 1 + PLANES - 1)

    def q_copy(d, slot):
        return remote(q_tiles.at[d], q_got.at[slot], qk_send.at[d], qk_recv.at[slot], kvh=d)

    def k_copy(d, slot):
        columns = pl.ds(pl.multiple_of(d * HEAD, HEAD), HEAD)
        return remote(k_hbm.at[:, columns], k_all.at[slot], kk_send.at[d], kk_recv.at[slot], kvh=d)

    others(KVH, k, lambda d: q_copy(d, k).start())
    others(KVH, k, lambda d: k_copy(d, k).start())
    others(KVH, k, lambda d: q_copy(d, d).wait_recv())

    q_flat[...] = q_got[...].astype(F32).reshape(KVH * 16, HEAD)
    for pair in range(16):
        q_turned[8 * pair : 8 * pair + 8, :] = q_flat[pl.ds(pair, 8, stride=16), :]
    q_own[...] = q_turned[...].astype(BF16).reshape(HEADS, 16, HEAD)
    q_all[:, s] = q_own[...]

    def q_round(d):
        return remote(q_own, q_all.at[:, s], qz_send.at[d], q_recv.at[s], seq=at_seq(y, d))

    def q_pass(piece, way, plane):
        return remote(
            q_all.at[:, piece], q_all.at[:, piece], qf_send.at[way, piece], q_recv.at[piece],
            seq=at_seq(plane, z),
        )

    def q_arrived(piece):
        remote(q_own, q_all.at[:, piece], qz_send.at[0], q_recv.at[piece], seq=piece).wait_recv()

    def q_rounds(step):
        def run(index):
            d = lax.rem(z + index, RING)

            @pl.when((y > 0) | (d == 0))
            def _():
                step(d)

        each(RING, run, 1)

    q_rounds(lambda d: q_round(d).start())

    def pass_block(block, own, targets, start):
        def run(index):
            piece = at_seq(block, lax.rem(z + index, RING))
            if start:
                if own:
                    @pl.when(index > 0)
                    def _():
                        q_arrived(piece)
                else:
                    q_arrived(piece)
            for way, plane in enumerate(targets):
                copy = q_pass(piece, way, plane)
                if start:
                    copy.start()
                else:
                    copy.wait_send()

        each(RING, run)

    def pass_all(start):
        @pl.when(y == 3)
        def _():
            pass_block(3, True, (0, 2), start)

        @pl.when(y == 2)
        def _():
            pass_block(2, True, (1,), start)

        @pl.when(y == 1)
        def _():
            pass_block(1, True, (0,), start)
            pass_block(2, False, (0,), start)

        @pl.when(y == 0)
        def _():
            pass_block(3, False, (1,), start)

    omega_copy.wait()
    for tile in range(4):
        turned = omega_rows[:, tile * 128 : (tile + 1) * 128].astype(F32).T.astype(BF16)
        omega_turned[2 * tile] = turned[:RANK]
        omega_turned[2 * tile + 1] = turned[RANK:]

    pass_all(True)
    keys_copy.wait()
    others(KVH, k, lambda d: k_copy(d, d).wait_recv())

    lane = lax.broadcasted_iota(jnp.int32, (1, BLOCK), 1)
    place = lax.rem(lane, 16)
    row_in_block = lane - place + 2 * lax.rem(place, 8) + lax.div(place, 8)
    key_row = lax.broadcasted_iota(jnp.int32, (CHUNK, 1), 0)

    def limits(block):
        return offsets[block] * BLOCK + row_in_block - s * KEYS

    def fold(tile, join):
        return join(tile.reshape(CHUNK // 8, 8, tile.shape[1]), axis=0)

    def head_at(index):
        turn = lax.div(index, 2)
        turn = jnp.where(turn < 2, turn, 5 - turn)
        plane = lax.rem(y + turn, PLANES)
        return plane, lax.rem(index, 2), 2 * plane + lax.rem(index, 2)

    def spans(plane, act, everything=False):
        if isinstance(plane, int):
            if plane:
                act(plane)
            elif everything:
                act(0)
            else:
                pl.when(z == 0)(lambda: act(0))
                pl.when(z != 0)(lambda: act(1))
        else:
            if everything:
                pl.when(plane == 0)(lambda: act(0))
                pl.when(plane == 1)(lambda: act(1))
            else:
                pl.when((plane == 0) & (z == 0))(lambda: act(0))
                pl.when((plane == 1) | ((plane == 0) & (z != 0)))(lambda: act(1))
            pl.when(plane == 2)(lambda: act(2))
            pl.when(plane == 3)(lambda: act(3))

    def cut(ref, *place, first):
        return ref.at[(*place, pl.ds(first, PLANES - first))]

    def y_send(out, landing, send, recv, head, plane, j, start):
        @pl.when(plane != y)
        def _():
            def act(first):
                copy = remote(
                    cut(out, head, first=first), cut(landing, y, j, first=first),
                    send.at[head], recv.at[y, j], seq=at_seq(plane, z),
                )
                if start:
                    copy.start()
                else:
                    copy.wait_send()

            spans(y, act)

    def y_wait(out, landing, send, recv, j):
        for plane in range(PLANES):
            @pl.when(plane != y)
            def _():
                def act(first):
                    remote(
                        cut(out, 0, first=first), cut(landing, plane, j, first=first),
                        send.at[0], recv.at[plane, j], seq=at_seq(plane, z),
                    ).wait_recv()

                spans(plane, act)

    def z_send(through, landing, send, recv, j, start):
        target = owner_z(j)

        @pl.when(target != z)
        def _():
            def act(first):
                copy = remote(
                    cut(through, j, first=first), cut(landing, z, first=first),
                    send.at[j], recv.at[z], seq=at_seq(y, target),
                )
                if start:
                    copy.start()
                else:
                    copy.wait_send()

            spans(0, act)

    def z_wait(through, landing, send, recv):
        def run(d):
            for first in (0, 1):
                @pl.when((d == 0) if first == 0 else (d != 0))
                def _():
                    remote(
                        cut(through, 0, first=first), cut(landing, d, first=first),
                        send.at[0], recv.at[d], seq=at_seq(y, d),
                    ).wait_recv()

        others(RING, z, run)

    def stat_y_copy(head, plane, j, source):
        return remote(
            stat_out.at[head], stat_y.at[source, j], sty_send.at[head], sty_recv.at[source, j],
            seq=at_seq(plane, z),
        )

    def first_block(block, columns, head):
        q_head = q_all[head, pl.ds(pl.multiple_of(8 * block, 8), 8)].reshape(BLOCK, HEAD)
        limit = limits(block)
        largest = jnp.full((8, BLOCK), LOWEST, F32)
        for chunk in range(KEYS // CHUNK):
            piece = dot(k_all[chunk], q_head, LANES)
            piece = jnp.where(key_row + chunk * CHUNK <= limit, piece, MASKED)
            scores[head, chunk * CHUNK : (chunk + 1) * CHUNK, columns] = piece
            largest = jnp.maximum(largest, fold(piece, jnp.max))
        top = jnp.max(largest, axis=0, keepdims=True)
        total = jnp.zeros((8, BLOCK), F32)
        for chunk in range(KEYS // CHUNK):
            at = slice(chunk * CHUNK, (chunk + 1) * CHUNK)
            weight = jnp.exp2((scores[head, at, columns] - top) * SCALE)
            total = total + fold(weight, jnp.sum)
            probs[head, at, columns] = weight.astype(BF16)
        place = pl.ds(pl.multiple_of(block * BLOCK, BLOCK), BLOCK)
        stat_out[head, 0:1, place] = top
        stat_out[head, 1:2, place] = jnp.sum(total, axis=0, keepdims=True)
        wide_out[head, block] = dot(omega_turned[head], probs[head, :, columns])

    def block_zero(head):
        q_head = q_all[head, 0:8].reshape(BLOCK, HEAD)
        piece = jnp.where(key_row <= limits(0), dot(k_all[0], q_head, LANES), MASKED)
        scores_first[head] = piece
        top = jnp.max(piece, axis=0, keepdims=True)
        weight = jnp.exp2((piece - top) * SCALE)
        probs_first[head] = weight.astype(BF16)
        stat_out[head, 0:1, :BLOCK] = top
        stat_out[head, 1:2, :BLOCK] = jnp.sum(weight, axis=0, keepdims=True)
        wide_out[head, 0] = dot(omega_turned[head, :, :BLOCK], probs_first[head])

    @pl.when(s == 0)
    def _():
        others(RING, z, q_arrived)
        each(HEADS, block_zero)

    steps = jnp.where(y == 0, 3, PLANES - y)

    def one_block(step):
        block = jnp.where(y == 0, jnp.where(step == 0, 3, step), y + step)
        columns = pl.ds(pl.multiple_of((block - 1) * BLOCK, BLOCK), BLOCK)

        @pl.when(jnp.where(y == 0, block != 3, (block == 3) & (y < 3)))
        def _():
            each(RING, lambda d: q_arrived(at_seq(block, d)))

        def run(index):
            plane, j, head = head_at(index)
            first_block(block, columns, head)

            @pl.when(step == steps - 1)
            def _():
                @pl.when(plane != y)
                def _():
                    stat_y_copy(head, plane, j, y).start()

                y_send(wide_out, wide_y, wy_send, wy_recv, head, plane, j, True)

                @pl.when(plane == y)
                def _():
                    wide_y[y, j] = wide_out[head]
                    stat_y[y, j] = stat_out[head]

        each(HEADS, run)

    each(steps, one_block)

    def merge_scale(value, top):
        return jnp.exp2((value - top) * SCALE)

    def block_of(row, block):
        return row[:, block * BLOCK : (block + 1) * BLOCK]

    def join_wide(j):
        for plane in range(PLANES):
            @pl.when(plane != y)
            def _():
                stat_y_copy(0, plane, j, plane).wait_recv()

        tops = [stat_y[p, j, 0:1, :] for p in range(PLANES)]
        top = functools.reduce(jnp.maximum, tops)
        scales = [merge_scale(value, top) for value in tops]
        stat_sum[j, 0:1, :] = top
        stat_sum[j, 1:2, :] = sum(stat_y[p, j, 1:2, :] * scales[p] for p in range(PLANES))

        @pl.when(owner_z(j) == z)
        def _():
            stat_z[z] = stat_sum[j]

        @pl.when(owner_z(j) != z)
        def _():
            stat_z_copy(j, z).start()

        y_wait(wide_out, wide_y, wy_send, wy_recv, j)
        for block in range(1, PLANES):
            wide_sum[j, block] = sum(
                wide_y[p, j, block] * block_of(scales[p], block) for p in range(block + 1)
            )

        @pl.when(z == 0)
        def _():
            wide_sum[j, 0] = wide_y[0, j, 0] * block_of(scales[0], 0)

        @pl.when(owner_z(j) == z)
        def _():
            wide_z[z] = wide_sum[j]

        z_send(wide_sum, wide_z, wz_send, wz_recv, j, True)

    def stat_z_copy(j, source):
        return remote(
            stat_sum.at[j], stat_z.at[source], stz_send.at[j], stz_recv.at[source],
            seq=at_seq(y, owner_z(j)),
        )

    join_wide(0)
    join_wide(1)

    def stat_share(d):
        return remote(
            stat_all.at[own_head], stat_all.at[own_head], sta_send.at[d], st_recv.at[own_head],
            seq=at_seq(y, d),
        )

    def basis_share(d):
        return remote(
            basis.at[own_head], basis.at[own_head], bz_send.at[d], b_recv.at[own_head],
            seq=at_seq(y, d),
        )

    def store_basis(rows):
        for block in range(PLANES):
            basis[own_head, block] = block_of(rows, block).astype(BF16)

    @pl.when(owns)
    def _():
        others(RING, z, lambda d: stat_z_copy(0, d).wait_recv())
        top = functools.reduce(jnp.maximum, [stat_z[d, 0:1, :] for d in range(RING)])
        scales = [merge_scale(stat_z[d, 0:1, :], top) for d in range(RING)]
        inverse = 1.0 / sum(stat_z[d, 1:2, :] * scales[d] for d in range(RING))
        stat_all[own_head, 0:1, :] = top
        stat_all[own_head, 1:2, :] = inverse
        others(RING, z, lambda d: stat_share(d).start())
        z_wait(wide_sum, wide_z, wz_send, wz_recv)
        pieces = [wide_z[0, 0] * block_of(scales[0], 0)]
        for block in range(1, PLANES):
            pieces.append(sum(wide_z[d, block] * block_of(scales[d], block) for d in range(RING)))
        store_basis(orthonormal_rows(jnp.concatenate(pieces, axis=1) * inverse))
        others(RING, z, lambda d: basis_share(d).start())

    def stat_pass(j, plane):
        head = 2 * y + j
        return remote(
            stat_all.at[head], stat_all.at[head], stb_send.at[j, plane], st_recv.at[head],
            seq=at_seq(plane, z),
        )

    def stat_wait(head):
        remote(stat_all.at[head], stat_all.at[head], sta_send.at[0], st_recv.at[head], seq=s).wait_recv()

    def relay_stats(j):
        @pl.when(owner_z(j) != z)
        def _():
            stat_wait(2 * y + j)

        others(PLANES, y, lambda plane: stat_pass(j, plane).start())

    def relay_basis(j, last, start):
        head = 2 * y + j
        if start:
            @pl.when(owner_z(j) != z)
            def _():
                remote(
                    basis.at[head], basis.at[head], bz_send.at[0], b_recv.at[head], seq=s
                ).wait_recv()

        for plane in range(PLANES):
            @pl.when(plane != y)
            def _():
                def act(first):
                    copy = remote(
                        cut(basis, head, first=first), cut(basis, head, first=first),
                        by_send.at[j, plane], b_recv.at[head], seq=at_seq(plane, z),
                    )
                    if start:
                        copy.start()
                    else:
                        copy.wait_send()

                spans(plane, act, last)

    def wait_basis(plane, head, last):
        @pl.when(plane != y)
        def _():
            def act(first):
                remote(
                    cut(basis, head, first=first), cut(basis, head, first=first),
                    by_send.at[0, 0], b_recv.at[head], seq=at_seq(plane, z),
                ).wait_recv()

            spans(y, act, last)

    relay_stats(0)
    relay_stats(1)

    def normalise(index):
        plane, j, head = head_at(index)

        @pl.when(plane != y)
        def _():
            stat_wait(head)

        def run(block):
            columns = pl.ds(pl.multiple_of((block - 1) * BLOCK, BLOCK), BLOCK)
            place = pl.ds(pl.multiple_of(block * BLOCK, BLOCK), BLOCK)
            top = stat_all[head, 0:1, place]
            inverse = stat_all[head, 1:2, place]
            for chunk in range(KEYS // CHUNK):
                at = slice(chunk * CHUNK, (chunk + 1) * CHUNK)
                weight = merge_scale(scores[head, at, columns], top)
                probs[head, at, columns] = (weight * inverse).astype(BF16)

        each(PLANES, run, jnp.maximum(y, 1))

        @pl.when(s == 0)
        def _():
            weight = merge_scale(scores_first[head], stat_all[head, 0:1, :BLOCK])
            probs_first[head] = (weight * stat_all[head, 1:2, :BLOCK]).astype(BF16)

    @pl.when(owns)
    def _():
        relay_basis(own_j, False, True)

    each(HEADS, normalise)

    def forward(head, plane, j, panel):
        product = dot(panel, probs[head]).astype(BF16)
        for b in range(3):
            part_out[head, b + 1] = product[:, b * BLOCK : (b + 1) * BLOCK]

        @pl.when(s == 0)
        def _():
            part_out[head, 0] = dot(panel[:, :BLOCK], probs_first[head]).astype(BF16)

        @pl.when(plane == y)
        def _():
            part_y[y, j] = part_out[head]

    def backward(head):
        low = jnp.concatenate([basis[head, 1], basis[head, 2], basis[head, 3]], axis=1)
        product = dot(low, probs[head], LANES)
        first = dot(basis[head, 0], probs_first[head], LANES)
        return jnp.concatenate([product[:, :BLOCK] + first, product[:, BLOCK:]], axis=1)

    def join_parts(j):
        y_wait(part_out, part_y, py_send, py_recv, j)
        relay_basis(j, False, False)
        for block in range(1, PLANES):
            part_sum[j, block] = sum(
                part_y[p, j, block].astype(F32) for p in range(block + 1)
            ).astype(BF16)

        @pl.when(z == 0)
        def _():
            part_sum[j, 0] = part_y[0, j, 0]

        @pl.when(owner_z(j) == z)
        def _():
            part_z[z] = part_sum[j]

        z_send(part_sum, part_z, pz_send, pz_recv, j, True)

    def start_relays(last, first_round):
        for j in range(2):
            if first_round is None:
                relay_basis(j, last, True)
            else:
                @pl.when(jnp.logical_not(first_round & (owner_z(j) == z)))
                def _():
                    relay_basis(j, last, True)

    def power_step(step):
        start_relays(False, step == 0)

        def one_head(index):
            plane, j, head = head_at(index)
            wait_basis(plane, head, False)
            forward(head, plane, j, backward(head).astype(BF16))
            y_send(part_out, part_y, py_send, py_recv, head, plane, j, True)

        each(HEADS, one_head)
        join_parts(0)
        join_parts(1)

        @pl.when(owns)
        def _():
            z_wait(part_sum, part_z, pz_send, pz_recv)
            pieces = [part_z[0, 0].astype(F32)]
            for block in range(1, PLANES):
                pieces.append(sum(part_z[d, block].astype(F32) for d in range(RING)))
            rows = orthonormal_rows(jnp.concatenate(pieces, axis=1))
            others(RING, z, lambda d: basis_share(d).wait_send())
            store_basis(rows)
            others(RING, z, lambda d: basis_share(d).start())

        def sent(index):
            plane, j, head = head_at(index)
            y_send(part_out, part_y, py_send, py_recv, head, plane, j, False)

        each(HEADS, sent)
        z_send(part_sum, part_z, pz_send, pz_recv, 0, False)
        z_send(part_sum, part_z, pz_send, pz_recv, 1, False)

    each(POWER, power_step)

    def store_copy(head):
        rows = pl.ds(pl.multiple_of(head * RANK, RANK), RANK)
        return pltpu.make_async_copy(staged.at[rows], proj_hbm.at[rows], store_sem.at[head])

    start_relays(True, None)

    def last_head(index):
        plane, j, head = head_at(index)
        wait_basis(plane, head, True)
        rows = pl.ds(pl.multiple_of(head * RANK, RANK), RANK)
        staged[rows, :] = backward(head) * math.sqrt(SEQ * KEYS)
        store_copy(head).start()

    each(HEADS, last_head)

    row = lax.broadcasted_iota(jnp.int32, (16, QUERIES), 0)
    lane = lax.broadcasted_iota(jnp.int32, (16, QUERIES), 1)
    chosen = lane == s * 16 + 8 * lax.rem(row, 2) + lax.div(row, 2)
    chosen = jnp.where(chosen, 1.0, 0.0).astype(BF16)
    total = jnp.zeros((16, HEADS * RANK), F32)
    for block in range(PLANES):
        total = total + dot(
            chosen[:, block * BLOCK : (block + 1) * BLOCK],
            basis[:, block].reshape(HEADS * RANK, BLOCK),
            LANES,
        )
    basis_ref[...] = total * math.sqrt(QUERIES)

    each(HEADS, lambda head: store_copy(head).wait())
    others(KVH, k, lambda d: q_copy(d, k).wait_send())
    others(KVH, k, lambda d: k_copy(d, k).wait_send())
    q_rounds(lambda d: q_round(d).wait_send())
    pass_all(False)

    def sent_wide(index):
        plane, j, head = head_at(index)

        @pl.when(plane != y)
        def _():
            stat_y_copy(head, plane, j, y).wait_send()

        y_send(wide_out, wide_y, wy_send, wy_recv, head, plane, j, False)

    each(HEADS, sent_wide)
    for j in range(2):
        z_send(wide_sum, wide_z, wz_send, wz_recv, j, False)

        @pl.when(owner_z(j) != z)
        def _():
            stat_z_copy(j, z).wait_send()

        others(PLANES, y, lambda plane: stat_pass(j, plane).wait_send())
        relay_basis(j, True, False)

    @pl.when(owns)
    def _():
        others(RING, z, lambda d: stat_share(d).wait_send())
        others(RING, z, lambda d: basis_share(d).wait_send())


def body(queries, keys, omega, block_offsets):
    vmem = lambda shape, kind: pltpu.VMEM(shape, kind)
    dma = lambda *shape: pltpu.SemaphoreType.DMA(shape)
    panel = (PLANES, RANK, BLOCK)
    return pl.pallas_call(
        kernel,
        out_shape=(
            jax.ShapeDtypeStruct((16, HEADS * RANK), F32),
            jax.ShapeDtypeStruct((HEADS * RANK, KEYS), F32),
        ),
        in_specs=[
            pl.BlockSpec(memory_space=pltpu.SMEM),
            pl.BlockSpec(memory_space=pltpu.VMEM),
            pl.BlockSpec(memory_space=pl.ANY),
            pl.BlockSpec(memory_space=pl.ANY),
        ],
        out_specs=(
            pl.BlockSpec(memory_space=pltpu.VMEM),
            pl.BlockSpec(memory_space=pl.ANY),
        ),
        scratch_shapes=[
            vmem((128, HEAD), F32),
            vmem((KVH, 16, HEAD), BF16),
            vmem((KVH, 16, HEAD), BF16),
            vmem((128, HEAD), F32),
            vmem((128, HEAD), F32),
            vmem((HEADS, 16, HEAD), BF16),
            vmem((HEADS, SEQ, 16, HEAD), BF16),
            vmem((KVH, 128, HEAD), BF16),
            vmem((KEYS, HEADS * RANK), BF16),
            vmem((HEADS, RANK, KEYS), BF16),
            vmem((HEADS, KEYS, WIDE), F32),
            vmem((HEADS, BLOCK, BLOCK), F32),
            vmem((HEADS, KEYS, WIDE), BF16),
            vmem((HEADS, BLOCK, BLOCK), BF16),
            vmem((HEADS, 2, QUERIES), F32),
            vmem((PLANES, 2, 2, QUERIES), F32),
            vmem((2, 2, QUERIES), F32),
            vmem((RING, 2, QUERIES), F32),
            vmem((HEADS, 2, QUERIES), F32),
            vmem((HEADS, *panel), F32),
            vmem((PLANES, 2, *panel), F32),
            vmem((2, *panel), F32),
            vmem((RING, *panel), F32),
            vmem((HEADS, *panel), BF16),
            vmem((PLANES, 2, *panel), BF16),
            vmem((2, *panel), BF16),
            vmem((RING, *panel), BF16),
            vmem((HEADS, *panel), BF16),
            vmem((HEADS * RANK, KEYS), F32),
            dma(2),
            dma(HEADS),
            dma(KVH), dma(KVH),
            dma(KVH), dma(KVH),
            dma(RING), dma(2, SEQ), dma(SEQ),
            dma(HEADS), dma(PLANES, 2),
            dma(2), dma(RING),
            dma(RING), dma(2, PLANES), dma(HEADS),
            dma(HEADS), dma(PLANES, 2),
            dma(2), dma(RING),
            dma(HEADS), dma(PLANES, 2),
            dma(2), dma(RING),
            dma(RING), dma(2, PLANES), dma(HEADS),
        ],
        compiler_params=pltpu.CompilerParams(
            collective_id=0, has_side_effects=True, vmem_limit_bytes=56 * 2**20
        ),
        cost_estimate=pl.CostEstimate(
            flops=6 * 10**9, bytes_accessed=8 * 2**20, transcendentals=8 * 10**6
        ),
        name="range_finder",
    )(block_offsets, queries, keys, omega)


def solution(mesh):
    placed = (P(("seq", "kvh"), None), P(("seq", "kvh"), None), P("seq", "kvh"), P())
    return jax.shard_map(
        body,
        mesh=mesh,
        in_specs=placed,
        out_specs=(P("seq", "kvh"), P("kvh", "seq")),
        check_vma=False,
    )
```

time: 160 us -> 136 us (0.85)
  Pallas kernels: 154 us -> 131 us
    pallas_call x1, Pallas kernels: 154 us -> 131 us  [body(): pl.pallas_call(kernel, out_shape=(jax.ShapeDtypeStruct((16, HEADS * RANK)...]
where the time goes in v2:
time: 136 us
  Pallas kernels  131 us (96%)
  local copies, waits for them, and re-layouts  4.53 us (3%)
    pallas_call x1, Pallas kernels, body(): pl.pallas_call(kernel, out_shape=(jax.ShapeDtypeStruct((16, HEADS * RANK)...  131 us
    unnamed x2, local copies, waits for them, and re-layouts  4.53 us

profile of v2, /device:TPU:24, one launch (start us, length us, event | category | flops | bytes accessed | tf_op | source)
XLA Modules:
  0.0 135.9 jit_solution(12629738290109753403)
XLA Ops:
  0.6 130.7 %range_finder.1 = (f32[16,512]{1,0:T(8,128)}, f32[512,1024]{1,0:T(8,128)}) custom-call(s32[4]{0:T(128)} %offsets.1, bf16[2,8192]{1,0:T(2,128)(2,1)} %q_ref.1, bf16[128,1024]{1,0:T(8,128)(2,1)} %k_hbm.1, bf16[1024,512]{1,0:T(8,128)(2,1)} %omega_hbm.1), custom_call_target="tpu_custom_call" | custom-call | flops 6000000000 | bytes 8388608 | tf_op jit(solution)/shard_map/range_finder/pallas_call | solution.py:801
  131.4 1.4 %copy.8 = f32[16,512]{1,0:T(8,128)} copy(f32[16,512]{1,0:T(8,128)} %get-tuple-element.4) | data formatting | bytes 65536
  132.8 3.2 %copy.9 = f32[512,1024]{1,0:T(8,128)} copy(f32[512,1024]{1,0:T(8,128)} %get-tuple-element.5) | data formatting | bytes 4194304

commit v3 on v2

--- a/solution.py
+++ b/solution.py
@@ -270,42 +270,61 @@
 
     q_rounds(lambda d: q_round(d).start())
 
-    def pass_block(block, own, targets, start):
+    def pass_block(block, own, step, start):
         def run(index):
-            piece = at_seq(block, lax.rem(z + index, RING))
+            place = lax.rem(z + index, RING)
+            piece = at_seq(block, place)
             if start:
                 if own:
-                    @pl.when(index > 0)
-                    def _():
-                        q_arrived(piece)
+                    pl.when(index > 0)(lambda: q_arrived(piece))
                 else:
                     q_arrived(piece)
-            for way, plane in enumerate(targets):
-                copy = q_pass(piece, way, plane)
+            step(piece, lax.rem(place, 2) == 1)
+
+        each(RING, run)
+
+    def pass_all(start):
+        def go(piece, way, plane):
+            copy = q_pass(piece, way, plane)
+            if start:
+                copy.start()
+            else:
+                copy.wait_send()
+
+        @pl.when(y == 3)
+        def _():
+            def both(piece, odd):
+                go(piece, 0, 0)
+                go(piece, 1, 2)
+
+            pass_block(3, True, both, start)
+
+            def other(index):
+                piece = at_seq(2, 2 * index + 1)
                 if start:
-                    copy.start()
-                else:
-                    copy.wait_send()
-
-        each(RING, run)
-
-    def pass_all(start):
-        @pl.when(y == 3)
-        def _():
-            pass_block(3, True, (0, 2), start)
+                    q_arrived(piece)
+                go(piece, 0, 0)
+
+            each(RING // 2, other)
 
         @pl.when(y == 2)
         def _():
-            pass_block(2, True, (1,), start)
+            def both(piece, odd):
+                pl.when(odd)(lambda: go(piece, 1, 3))
+                go(piece, 0, 1)
+
+            pass_block(2, True, both, start)
 
         @pl.when(y == 1)
         def _():
-            pass_block(1, True, (0,), start)
-            pass_block(2, False, (0,), start)
+            pass_block(1, True, lambda piece, odd: go(piece, 0, 0), start)
+            pass_block(
+                2, False, lambda piece, odd: pl.when(~odd)(lambda: go(piece, 0, 0)), start
+            )
 
         @pl.when(y == 0)
         def _():
-            pass_block(3, False, (1,), start)
+            pass_block(3, False, lambda piece, odd: go(piece, 0, 1), start)
 
     omega_copy.wait()
     for tile in range(4):
@@ -322,6 +341,9 @@
     row_in_block = lane - place + 2 * lax.rem(place, 8) + lax.div(place, 8)
     key_row = lax.broadcasted_iota(jnp.int32, (CHUNK, 1), 0)
 
+    def block_of(row, block):
+        return row[:, block * BLOCK : (block + 1) * BLOCK]
+
     def limits(block):
         return offsets[block] * BLOCK + row_in_block - s * KEYS
 
@@ -329,10 +351,11 @@
         return join(tile.reshape(CHUNK // 8, 8, tile.shape[1]), axis=0)
 
     def head_at(index):
-        turn = lax.div(index, 2)
+        turn = lax.rem(index, 4)
         turn = jnp.where(turn < 2, turn, 5 - turn)
         plane = lax.rem(y + turn, PLANES)
-        return plane, lax.rem(index, 2), 2 * plane + lax.rem(index, 2)
+        j = lax.div(index, 4)
+        return plane, j, 2 * plane + j
 
     def spans(plane, act, everything=False):
         if isinstance(plane, int):
@@ -418,26 +441,32 @@
             seq=at_seq(plane, z),
         )
 
-    def first_block(block, columns, head):
-        q_head = q_all[head, pl.ds(pl.multiple_of(8 * block, 8), 8)].reshape(BLOCK, HEAD)
+    def first_block(block, columns, heads):
+        rows = pl.ds(pl.multiple_of(8 * block, 8), 8)
+        q_heads = jnp.concatenate([q_all[h, rows].reshape(BLOCK, HEAD) for h in heads], axis=0)
         limit = limits(block)
-        largest = jnp.full((8, BLOCK), LOWEST, F32)
+        limit = jnp.concatenate([limit, limit], axis=1)
+        largest = jnp.full((8, 2 * BLOCK), LOWEST, F32)
         for chunk in range(KEYS // CHUNK):
-            piece = dot(k_all[chunk], q_head, LANES)
+            at = slice(chunk * CHUNK, (chunk + 1) * CHUNK)
+            piece = dot(k_all[chunk], q_heads, LANES)
             piece = jnp.where(key_row + chunk * CHUNK <= limit, piece, MASKED)
-            scores[head, chunk * CHUNK : (chunk + 1) * CHUNK, columns] = piece
+            for n, head in enumerate(heads):
+                scores[head, at, columns] = block_of(piece, n)
             largest = jnp.maximum(largest, fold(piece, jnp.max))
         top = jnp.max(largest, axis=0, keepdims=True)
-        total = jnp.zeros((8, BLOCK), F32)
+        totals = [jnp.zeros((8, BLOCK), F32) for _ in heads]
         for chunk in range(KEYS // CHUNK):
             at = slice(chunk * CHUNK, (chunk + 1) * CHUNK)
-            weight = jnp.exp2((scores[head, at, columns] - top) * SCALE)
-            total = total + fold(weight, jnp.sum)
-            probs[head, at, columns] = weight.astype(BF16)
+            for n, head in enumerate(heads):
+                weight = jnp.exp2((scores[head, at, columns] - block_of(top, n)) * SCALE)
+                totals[n] = totals[n] + fold(weight, jnp.sum)
+                probs[head, at, columns] = weight.astype(BF16)
         place = pl.ds(pl.multiple_of(block * BLOCK, BLOCK), BLOCK)
-        stat_out[head, 0:1, place] = top
-        stat_out[head, 1:2, place] = jnp.sum(total, axis=0, keepdims=True)
-        wide_out[head, block] = dot(omega_turned[head], probs[head, :, columns])
+        for n, head in enumerate(heads):
+            stat_out[head, 0:1, place] = block_of(top, n)
+            stat_out[head, 1:2, place] = jnp.sum(totals[n], axis=0, keepdims=True)
+            wide_out[head, block] = dot(omega_turned[head], probs[head, :, columns])
 
     def block_zero(head):
         q_head = q_all[head, 0:8].reshape(BLOCK, HEAD)
@@ -465,32 +494,33 @@
         def _():
             each(RING, lambda d: q_arrived(at_seq(block, d)))
 
-        def run(index):
-            plane, j, head = head_at(index)
-            first_block(block, columns, head)
+        def run(pair):
+            two = [head_at(2 * pair), head_at(2 * pair + 1)]
+            first_block(block, columns, [head for _, _, head in two])
 
             @pl.when(step == steps - 1)
             def _():
-                @pl.when(plane != y)
-                def _():
-                    stat_y_copy(head, plane, j, y).start()
-
-                y_send(wide_out, wide_y, wy_send, wy_recv, head, plane, j, True)
-
-                @pl.when(plane == y)
-                def _():
-                    wide_y[y, j] = wide_out[head]
-                    stat_y[y, j] = stat_out[head]
-
-        each(HEADS, run)
+                for plane, j, head in two:
+                    send_first(plane, j, head)
+
+        def send_first(plane, j, head):
+            @pl.when(plane != y)
+            def _():
+                stat_y_copy(head, plane, j, y).start()
+
+            y_send(wide_out, wide_y, wy_send, wy_recv, head, plane, j, True)
+
+            @pl.when(plane == y)
+            def _():
+                wide_y[y, j] = wide_out[head]
+                stat_y[y, j] = stat_out[head]
+
+        each(HEADS // 2, run)
 
     each(steps, one_block)
 
     def merge_scale(value, top):
         return jnp.exp2((value - top) * SCALE)
-
-    def block_of(row, block):
-        return row[:, block * BLOCK : (block + 1) * BLOCK]
 
     def join_wide(j):
         for plane in range(PLANES):
@@ -534,27 +564,38 @@
             seq=at_seq(y, owner_z(j)),
         )
 
-    join_wide(0)
-    join_wide(1)
-
     def stat_share(d):
         return remote(
             stat_all.at[own_head], stat_all.at[own_head], sta_send.at[d], st_recv.at[own_head],
             seq=at_seq(y, d),
         )
 
-    def basis_share(d):
-        return remote(
-            basis.at[own_head], basis.at[own_head], bz_send.at[d], b_recv.at[own_head],
-            seq=at_seq(y, d),
-        )
+    def around(d, everything, act):
+        whole = (d == 0) | everything
+        pl.when(whole)(lambda: act(0))
+        pl.when(~whole)(lambda: act(1))
+
+    def share_basis(everything, start):
+        def run(d):
+            def act(first):
+                copy = remote(
+                    cut(basis, own_head, first=first), cut(basis, own_head, first=first),
+                    bz_send.at[d], b_recv.at[own_head], seq=at_seq(y, d),
+                )
+                if start:
+                    copy.start()
+                else:
+                    copy.wait_send()
+
+            around(d, everything, act)
+
+        others(RING, z, run)
 
     def store_basis(rows):
         for block in range(PLANES):
             basis[own_head, block] = block_of(rows, block).astype(BF16)
 
-    @pl.when(owns)
-    def _():
+    def own_wide():
         others(RING, z, lambda d: stat_z_copy(0, d).wait_recv())
         top = functools.reduce(jnp.maximum, [stat_z[d, 0:1, :] for d in range(RING)])
         scales = [merge_scale(stat_z[d, 0:1, :], top) for d in range(RING)]
@@ -567,7 +608,13 @@
         for block in range(1, PLANES):
             pieces.append(sum(wide_z[d, block] * block_of(scales[d], block) for d in range(RING)))
         store_basis(orthonormal_rows(jnp.concatenate(pieces, axis=1) * inverse))
-        others(RING, z, lambda d: basis_share(d).start())
+        share_basis(False, True)
+
+    def finish_wide(j):
+        join_wide(j)
+        pl.when(owns & (own_j == j))(own_wide)
+
+    each(2, finish_wide)
 
     def stat_pass(j, plane):
         head = 2 * y + j
@@ -591,9 +638,13 @@
         if start:
             @pl.when(owner_z(j) != z)
             def _():
-                remote(
-                    basis.at[head], basis.at[head], bz_send.at[0], b_recv.at[head], seq=s
-                ).wait_recv()
+                def arrived(first):
+                    remote(
+                        cut(basis, head, first=first), cut(basis, head, first=first),
+                        bz_send.at[0], b_recv.at[head], seq=s,
+                    ).wait_recv()
+
+                around(z, last, arrived)
 
         for plane in range(PLANES):
             @pl.when(plane != y)
@@ -691,38 +742,36 @@
 
         z_send(part_sum, part_z, pz_send, pz_recv, j, True)
 
-    def start_relays(last, first_round):
-        for j in range(2):
-            if first_round is None:
-                relay_basis(j, last, True)
-            else:
-                @pl.when(jnp.logical_not(first_round & (owner_z(j) == z)))
-                def _():
-                    relay_basis(j, last, True)
+    def own_parts(step):
+        z_wait(part_sum, part_z, pz_send, pz_recv)
+        pieces = [part_z[0, 0].astype(F32)]
+        for block in range(1, PLANES):
+            pieces.append(sum(part_z[d, block].astype(F32) for d in range(RING)))
+        rows = orthonormal_rows(jnp.concatenate(pieces, axis=1))
+        share_basis(False, False)
+        store_basis(rows)
+        share_basis(step == POWER - 1, True)
 
     def power_step(step):
-        start_relays(False, step == 0)
-
-        def one_head(index):
-            plane, j, head = head_at(index)
-            wait_basis(plane, head, False)
-            forward(head, plane, j, backward(head).astype(BF16))
-            y_send(part_out, part_y, py_send, py_recv, head, plane, j, True)
-
-        each(HEADS, one_head)
-        join_parts(0)
-        join_parts(1)
-
-        @pl.when(owns)
-        def _():
-            z_wait(part_sum, part_z, pz_send, pz_recv)
-            pieces = [part_z[0, 0].astype(F32)]
-            for block in range(1, PLANES):
-                pieces.append(sum(part_z[d, block].astype(F32) for d in range(RING)))
-            rows = orthonormal_rows(jnp.concatenate(pieces, axis=1))
-            others(RING, z, lambda d: basis_share(d).wait_send())
-            store_basis(rows)
-            others(RING, z, lambda d: basis_share(d).start())
+        def group(j):
+            @pl.when(~((step == 0) & (owner_z(j) == z)))
+            def _():
+                relay_basis(j, False, True)
+
+            def one_head(turn):
+                plane, _, head = head_at(4 * j + turn)
+                wait_basis(plane, head, False)
+                forward(head, plane, j, backward(head).astype(BF16))
+                y_send(part_out, part_y, py_send, py_recv, head, plane, j, True)
+
+            each(PLANES, one_head)
+
+        def finish(j):
+            join_parts(j)
+            pl.when(owns & (own_j == j))(lambda: own_parts(step))
+
+        each(2, group)
+        each(2, finish)
 
         def sent(index):
             plane, j, head = head_at(index)
@@ -738,16 +787,19 @@
         rows = pl.ds(pl.multiple_of(head * RANK, RANK), RANK)
         return pltpu.make_async_copy(staged.at[rows], proj_hbm.at[rows], store_sem.at[head])
 
-    start_relays(True, None)
-
-    def last_head(index):
-        plane, j, head = head_at(index)
-        wait_basis(plane, head, True)
-        rows = pl.ds(pl.multiple_of(head * RANK, RANK), RANK)
-        staged[rows, :] = backward(head) * math.sqrt(SEQ * KEYS)
-        store_copy(head).start()
-
-    each(HEADS, last_head)
+    def last_group(j):
+        relay_basis(j, True, True)
+
+        def last_head(turn):
+            plane, _, head = head_at(4 * j + turn)
+            wait_basis(plane, head, True)
+            rows = pl.ds(pl.multiple_of(head * RANK, RANK), RANK)
+            staged[rows, :] = backward(head)
+            store_copy(head).start()
+
+        each(PLANES, last_head)
+
+    each(2, last_group)
 
     row = lax.broadcasted_iota(jnp.int32, (16, QUERIES), 0)
     lane = lax.broadcasted_iota(jnp.int32, (16, QUERIES), 1)
@@ -760,7 +812,7 @@
             basis[:, block].reshape(HEADS * RANK, BLOCK),
             LANES,
         )
-    basis_ref[...] = total * math.sqrt(QUERIES)
+    basis_ref[...] = total
 
     each(HEADS, lambda head: store_copy(head).wait())
     others(KVH, k, lambda d: q_copy(d, k).wait_send())
@@ -791,14 +843,14 @@
     @pl.when(owns)
     def _():
         others(RING, z, lambda d: stat_share(d).wait_send())
-        others(RING, z, lambda d: basis_share(d).wait_send())
+        share_basis(True, False)
 
 
 def body(queries, keys, omega, block_offsets):
     vmem = lambda shape, kind: pltpu.VMEM(shape, kind)
     dma = lambda *shape: pltpu.SemaphoreType.DMA(shape)
     panel = (PLANES, RANK, BLOCK)
-    return pl.pallas_call(
+    basis, projection = pl.pallas_call(
         kernel,
         out_shape=(
             jax.ShapeDtypeStruct((16, HEADS * RANK), F32),
@@ -866,6 +918,7 @@
         ),
         name="range_finder",
     )(block_offsets, queries, keys, omega)
+    return basis * math.sqrt(QUERIES), projection * math.sqrt(SEQ * KEYS)
 
 
 def solution(mesh):

time: 136 us -> 151 us (1.11)
  Pallas kernels: 131 us -> 145 us
  other arithmetic: 0 us -> 4.67 us
  local copies, waits for them, and re-layouts: 4.53 us -> 0 us
    pallas_call x1, Pallas kernels: 131 us -> 145 us  [body(): pl.pallas_call(kernel, out_shape=(jax.ShapeDtypeStruct((16, HEADS * RANK)...]
    mul x0 -> x2, other arithmetic: none -> 4.67 us  [body(): return (basis * math.sqrt(QUERIES), projection * math.sqrt(SEQ * KEYS))]
    unnamed x2 -> x0, local copies, waits for them, and re-layouts: 4.53 us -> none
where the time goes in v3:
time: 151 us; the launch traced here: 150 us
  Pallas kernels  145 us (96%)
  other arithmetic  4.67 us (3%)
    pallas_call x1, Pallas kernels, body(): pl.pallas_call(kernel, out_shape=(jax.ShapeDtypeStruct((16, HEADS * RANK)...  145 us
    mul x2, other arithmetic, body(): return (basis * math.sqrt(QUERIES), projection * math.sqrt(SEQ * KEYS))  4.67 us

profile of v3, /device:TPU:24, one launch (start us, length us, event | category | flops | bytes accessed | tf_op | source)
XLA Modules:
  0.0 150.4 jit_solution(8812920487768545337)
XLA Ops:
  0.6 145.0 %range_finder.1 = (f32[16,512]{1,0:T(8,128)}, f32[512,1024]{1,0:T(8,128)}) custom-call(s32[4]{0:T(128)} %offsets.1, bf16[2,8192]{1,0:T(2,128)(2,1)} %q_ref.1, bf16[128,1024]{1,0:T(8,128)(2,1)} %k_hbm.1, bf16[1024,512]{1,0:T(8,128)(2,1)} %omega_hbm.1), custom_call_target="tpu_custom_call" | custom-call | flops 6000000000 | bytes 8388608 | tf_op jit(solution)/shard_map/range_finder/pallas_call | solution.py:853
  145.7 1.4 broadcast_multiply_fusion.1
  147.1 3.3 %broadcast_multiply_fusion = f32[512,1024]{1,0:T(8,128)} fusion(f32[512,1024]{1,0:T(8,128)} %get-tuple-element.5), kind=kLoop, calls=%fused_computation | loop fusion | flops 524288 | bytes 4194304 | tf_op jit(solution)/shard_map/mul | solution.py:921

commit v4 on v3

--- a/solution.py
+++ b/solution.py
@@ -59,9 +59,10 @@
     def lift(tile, row):
         return jnp.broadcast_to(tile[row : row + 1, :], tile.shape)
 
-    def block(step, tiles):
-        pivot = tiles[0]
-        columns = [spread(pivot, j) for j in range(8)]
+    tiles = [start[8 * i : 8 * i + 8] for i in range(8)]
+    for step in range(8):
+        pivot = tiles[step]
+        columns = [spread(pivot, 8 * step + j) for j in range(8)]
         inverses, upper, roots = [], [], jnp.zeros_like(pivot)
         for j in range(8):
             diagonal = lift(columns[j], j)
@@ -76,22 +77,17 @@
                 columns[other] = columns[other] - factor * across[other]
             upper.append(across)
         pivot_rows = [lift(pivot, j) for j in range(8)]
-        later = []
-        for index in range(1, 8):
+        for index in range(step + 1, 8):
             tile = tiles[index]
-            live = jnp.where(step + index < 8, 1.0, 0.0)
-            columns = [spread(tile, j) * live for j in range(8)]
+            columns = [spread(tile, 8 * step + j) for j in range(8)]
             for j in range(8):
                 factor = columns[j] * inverses[j]
                 tile = tile - factor * pivot_rows[j]
                 for other in range(j + 1, 8):
                     columns[other] = columns[other] - factor * upper[j][other]
-            later.append(tile)
-        later.append(pivot * roots)
-        return tuple(pltpu.roll(tile, 2 * RANK - 8, 1) for tile in later)
-
-    tiles = lax.fori_loop(0, 8, block, tuple(start[8 * i : 8 * i + 8] for i in range(8)))
-    return jnp.concatenate(tiles, axis=0)[:, :RANK]
+            tiles[index] = tile
+        tiles[step] = pivot * roots
+    return jnp.concatenate(tiles, axis=0)[:, RANK:]
 
 
 def orthonormal_rows(panel):
@@ -351,10 +347,8 @@
         return join(tile.reshape(CHUNK // 8, 8, tile.shape[1]), axis=0)
 
     def head_at(index):
-        turn = lax.rem(index, 4)
-        turn = jnp.where(turn < 2, turn, 5 - turn)
-        plane = lax.rem(y + turn, PLANES)
-        j = lax.div(index, 4)
+        plane = lax.rem(y + lax.div(index, 2), PLANES)
+        j = lax.rem(index, 2)
         return plane, j, 2 * plane + j
 
     def spans(plane, act, everything=False):
@@ -445,8 +439,8 @@
         rows = pl.ds(pl.multiple_of(8 * block, 8), 8)
         q_heads = jnp.concatenate([q_all[h, rows].reshape(BLOCK, HEAD) for h in heads], axis=0)
         limit = limits(block)
-        limit = jnp.concatenate([limit, limit], axis=1)
-        largest = jnp.full((8, 2 * BLOCK), LOWEST, F32)
+        limit = jnp.concatenate([limit] * len(heads), axis=1)
+        largest = jnp.full((8, len(heads) * BLOCK), LOWEST, F32)
         for chunk in range(KEYS // CHUNK):
             at = slice(chunk * CHUNK, (chunk + 1) * CHUNK)
             piece = dot(k_all[chunk], q_heads, LANES)
@@ -495,7 +489,7 @@
             each(RING, lambda d: q_arrived(at_seq(block, d)))
 
         def run(pair):
-            two = [head_at(2 * pair), head_at(2 * pair + 1)]
+            two = [head_at(4 * pair + n) for n in range(4)]
             first_block(block, columns, [head for _, _, head in two])
 
             @pl.when(step == steps - 1)
@@ -515,7 +509,7 @@
                 wide_y[y, j] = wide_out[head]
                 stat_y[y, j] = stat_out[head]
 
-        each(HEADS // 2, run)
+        each(HEADS // 4, run)
 
     each(steps, one_block)
 
@@ -610,11 +604,8 @@
         store_basis(orthonormal_rows(jnp.concatenate(pieces, axis=1) * inverse))
         share_basis(False, True)
 
-    def finish_wide(j):
-        join_wide(j)
-        pl.when(owns & (own_j == j))(own_wide)
-
-    each(2, finish_wide)
+    each(2, join_wide)
+    pl.when(owns)(own_wide)
 
     def stat_pass(j, plane):
         head = 2 * y + j
@@ -753,25 +744,21 @@
         share_basis(step == POWER - 1, True)
 
     def power_step(step):
-        def group(j):
+        def relay(j):
             @pl.when(~((step == 0) & (owner_z(j) == z)))
             def _():
                 relay_basis(j, False, True)
 
-            def one_head(turn):
-                plane, _, head = head_at(4 * j + turn)
-                wait_basis(plane, head, False)
-                forward(head, plane, j, backward(head).astype(BF16))
-                y_send(part_out, part_y, py_send, py_recv, head, plane, j, True)
-
-            each(PLANES, one_head)
-
-        def finish(j):
-            join_parts(j)
-            pl.when(owns & (own_j == j))(lambda: own_parts(step))
-
-        each(2, group)
-        each(2, finish)
+        def one_head(index):
+            plane, j, head = head_at(index)
+            wait_basis(plane, head, False)
+            forward(head, plane, j, backward(head).astype(BF16))
+            y_send(part_out, part_y, py_send, py_recv, head, plane, j, True)
+
+        each(2, relay)
+        each(HEADS, one_head)
+        each(2, join_parts)
+        pl.when(owns)(lambda: own_parts(step))
 
         def sent(index):
             plane, j, head = head_at(index)
@@ -787,19 +774,16 @@
         rows = pl.ds(pl.multiple_of(head * RANK, RANK), RANK)
         return pltpu.make_async_copy(staged.at[rows], proj_hbm.at[rows], store_sem.at[head])
 
-    def last_group(j):
-        relay_basis(j, True, True)
-
-        def last_head(turn):
-            plane, _, head = head_at(4 * j + turn)
-            wait_basis(plane, head, True)
-            rows = pl.ds(pl.multiple_of(head * RANK, RANK), RANK)
-            staged[rows, :] = backward(head)
-            store_copy(head).start()
-
-        each(PLANES, last_head)
-
-    each(2, last_group)
+    each(2, lambda j: relay_basis(j, True, True))
+
+    def last_head(index):
+        plane, j, head = head_at(index)
+        wait_basis(plane, head, True)
+        rows = pl.ds(pl.multiple_of(head * RANK, RANK), RANK)
+        staged[rows, :] = backward(head)
+        store_copy(head).start()
+
+    each(HEADS, last_head)
 
     row = lax.broadcasted_iota(jnp.int32, (16, QUERIES), 0)
     lane = lax.broadcasted_iota(jnp.int32, (16, QUERIES), 1)

time: 151 us -> 128 us (0.85); the launches traced: 150 us -> 125 us
  Pallas kernels: 145 us -> 120 us
    pallas_call x1, Pallas kernels: 145 us -> 120 us  [body(): pl.pallas_call(kernel, out_shape=(jax.ShapeDtypeStruct((16, HEADS * RANK)...]
where the time goes in v4:
time: 128 us; the launch traced here: 125 us
  Pallas kernels  120 us (94%)
  other arithmetic  4.67 us (4%)
    pallas_call x1, Pallas kernels, body(): pl.pallas_call(kernel, out_shape=(jax.ShapeDtypeStruct((16, HEADS * RANK)...  120 us
    mul x2, other arithmetic, body(): return (basis * math.sqrt(QUERIES), projection * math.sqrt(SEQ * KEYS))  4.67 us

profile of v4, /device:TPU:24, one launch (start us, length us, event | category | flops | bytes accessed | tf_op | source)
XLA Modules:
  0.0 125.2 jit_solution(17820799176062442222)
XLA Ops:
  0.6 119.9 %range_finder.1 = (f32[16,512]{1,0:T(8,128)}, f32[512,1024]{1,0:T(8,128)}) custom-call(s32[4]{0:T(128)} %offsets.1, bf16[2,8192]{1,0:T(2,128)(2,1)} %q_ref.1, bf16[128,1024]{1,0:T(8,128)(2,1)} %k_hbm.1, bf16[1024,512]{1,0:T(8,128)(2,1)} %omega_hbm.1), custom_call_target="tpu_custom_call" | custom-call | flops 6000000000 | bytes 8388608 | tf_op jit(solution)/shard_map/range_finder/pallas_call | solution.py:837
  120.6 1.4 %broadcast_multiply_fusion.1 = f32[16,512]{1,0:T(8,128)} fusion(f32[16,512]{1,0:T(8,128)} %get-tuple-element.4), kind=kLoop, calls=%fused_computation.1 | loop fusion | flops 8192 | bytes 65536 | tf_op jit(solution)/shard_map/mul | solution.py:905
  121.9 3.3 %broadcast_multiply_fusion = f32[512,1024]{1,0:T(8,128)} fusion(f32[512,1024]{1,0:T(8,128)} %get-tuple-element.5), kind=kLoop, calls=%fused_computation | loop fusion | flops 524288 | bytes 4194304 | tf_op jit(solution)/shard_map/mul | solution.py:905

commit v5 on v4

--- a/solution.py
+++ b/solution.py
@@ -96,11 +96,11 @@
 
 
 def kernel(
-    offsets,
-    q_ref,
+    offsets_hbm,
+    q_hbm,
     k_hbm,
     omega_hbm,
-    basis_ref,
+    basis_hbm,
     proj_hbm,
     q_wide,
     q_tiles,
@@ -131,6 +131,9 @@
     part_z,
     basis,
     staged,
+    chosen_rows,
+    offsets,
+    q_ref,
     local_sem,
     store_sem,
     qk_send,
@@ -189,14 +192,20 @@
 
         each(count, run)
 
+    offsets_copy = pltpu.make_async_copy(offsets_hbm, offsets, local_sem.at[2])
+    q_copy_in = pltpu.make_async_copy(q_hbm, q_ref, local_sem.at[3])
+    q_copy_in.start()
+    offsets_copy.start()
     barrier = pltpu.get_barrier_semaphore()
 
     def greet(**target):
         pl.semaphore_signal(barrier, inc=1, device_id=target, device_id_type=MESH)
 
+    for hop in (4, 3, 5, 2, 6, 1, 7):
+        greet(seq=at_seq(y, lax.rem(z + hop, RING)))
+    for hop in (2, 1, 3):
+        greet(seq=at_seq(lax.rem(y + hop, PLANES), z))
     others(KVH, k, lambda d: greet(kvh=d))
-    others(RING, z, lambda d: greet(seq=at_seq(y, d)))
-    others(PLANES, y, lambda d: greet(seq=at_seq(d, z)))
 
     omega_copy = pltpu.make_async_copy(omega_hbm, omega_rows, local_sem.at[0])
     omega_copy.start()
@@ -205,6 +214,8 @@
     )
     keys_copy.start()
 
+    q_copy_in.wait()
+    offsets_copy.wait()
     q_now = q_ref[...].astype(F32)
     for tile in range(KVH * HEADS):
         q_wide[2 * tile : 2 * tile + 2, :] = q_now[:, tile * HEAD : (tile + 1) * HEAD]
@@ -352,21 +363,16 @@
         return plane, j, 2 * plane + j
 
     def spans(plane, act, everything=False):
+        whole = (z == 0) | everything
         if isinstance(plane, int):
             if plane:
                 act(plane)
-            elif everything:
-                act(0)
             else:
-                pl.when(z == 0)(lambda: act(0))
-                pl.when(z != 0)(lambda: act(1))
+                pl.when(whole)(lambda: act(0))
+                pl.when(~whole)(lambda: act(1))
         else:
-            if everything:
-                pl.when(plane == 0)(lambda: act(0))
-                pl.when(plane == 1)(lambda: act(1))
-            else:
-                pl.when((plane == 0) & (z == 0))(lambda: act(0))
-                pl.when((plane == 1) | ((plane == 0) & (z != 0)))(lambda: act(1))
+            pl.when((plane == 0) & whole)(lambda: act(0))
+            pl.when((plane == 1) | ((plane == 0) & ~whole))(lambda: act(1))
             pl.when(plane == 2)(lambda: act(2))
             pl.when(plane == 3)(lambda: act(3))
 
@@ -435,7 +441,7 @@
             seq=at_seq(plane, z),
         )
 
-    def first_block(block, columns, heads):
+    def first_block(block, columns, heads, masked):
         rows = pl.ds(pl.multiple_of(8 * block, 8), 8)
         q_heads = jnp.concatenate([q_all[h, rows].reshape(BLOCK, HEAD) for h in heads], axis=0)
         limit = limits(block)
@@ -444,7 +450,8 @@
         for chunk in range(KEYS // CHUNK):
             at = slice(chunk * CHUNK, (chunk + 1) * CHUNK)
             piece = dot(k_all[chunk], q_heads, LANES)
-            piece = jnp.where(key_row + chunk * CHUNK <= limit, piece, MASKED)
+            if masked:
+                piece = jnp.where(key_row + chunk * CHUNK <= limit, piece, MASKED)
             for n, head in enumerate(heads):
                 scores[head, at, columns] = block_of(piece, n)
             largest = jnp.maximum(largest, fold(piece, jnp.max))
@@ -490,7 +497,9 @@
 
         def run(pair):
             two = [head_at(4 * pair + n) for n in range(4)]
-            first_block(block, columns, [head for _, _, head in two])
+            heads = [head for _, _, head in two]
+            pl.when(block == y)(lambda: first_block(block, columns, heads, True))
+            pl.when(block != y)(lambda: first_block(block, columns, heads, False))
 
             @pl.when(step == steps - 1)
             def _():
@@ -742,12 +751,40 @@
         share_basis(False, False)
         store_basis(rows)
         share_basis(step == POWER - 1, True)
+        relay_basis(own_j, step == POWER - 1, True)
+
+    def settle():
+        others(KVH, k, lambda d: q_copy(d, k).wait_send())
+        others(KVH, k, lambda d: k_copy(d, k).wait_send())
+        q_rounds(lambda d: q_round(d).wait_send())
+        pass_all(False)
+
+        def sent_wide(index):
+            plane, j, head = head_at(index)
+
+            @pl.when(plane != y)
+            def _():
+                stat_y_copy(head, plane, j, y).wait_send()
+
+            y_send(wide_out, wide_y, wy_send, wy_recv, head, plane, j, False)
+
+        each(HEADS, sent_wide)
+        for j in range(2):
+            z_send(wide_sum, wide_z, wz_send, wz_recv, j, False)
+
+            @pl.when(owner_z(j) != z)
+            def _():
+                stat_z_copy(j, z).wait_send()
+
+            others(PLANES, y, lambda plane: stat_pass(j, plane).wait_send())
+
+        @pl.when(owns)
+        def _():
+            others(RING, z, lambda d: stat_share(d).wait_send())
 
     def power_step(step):
         def relay(j):
-            @pl.when(~((step == 0) & (owner_z(j) == z)))
-            def _():
-                relay_basis(j, False, True)
+            pl.when(owner_z(j) != z)(lambda: relay_basis(j, False, True))
 
         def one_head(index):
             plane, j, head = head_at(index)
@@ -767,6 +804,7 @@
         each(HEADS, sent)
         z_send(part_sum, part_z, pz_send, pz_recv, 0, False)
         z_send(part_sum, part_z, pz_send, pz_recv, 1, False)
+        pl.when(step == 0)(settle)
 
     each(POWER, power_step)
 
@@ -774,7 +812,10 @@
         rows = pl.ds(pl.multiple_of(head * RANK, RANK), RANK)
         return pltpu.make_async_copy(staged.at[rows], proj_hbm.at[rows], store_sem.at[head])
 
-    each(2, lambda j: relay_basis(j, True, True))
+    def last_relay(j):
+        pl.when(owner_z(j) != z)(lambda: relay_basis(j, True, True))
+
+    each(2, last_relay)
 
     def last_head(index):
         plane, j, head = head_at(index)
@@ -796,38 +837,15 @@
             basis[:, block].reshape(HEADS * RANK, BLOCK),
             LANES,
         )
-    basis_ref[...] = total
+    chosen_rows[...] = total
+    basis_copy = pltpu.make_async_copy(chosen_rows, basis_hbm, local_sem.at[0])
+    basis_copy.start()
 
     each(HEADS, lambda head: store_copy(head).wait())
-    others(KVH, k, lambda d: q_copy(d, k).wait_send())
-    others(KVH, k, lambda d: k_copy(d, k).wait_send())
-    q_rounds(lambda d: q_round(d).wait_send())
-    pass_all(False)
-
-    def sent_wide(index):
-        plane, j, head = head_at(index)
-
-        @pl.when(plane != y)
-        def _():
-            stat_y_copy(head, plane, j, y).wait_send()
-
-        y_send(wide_out, wide_y, wy_send, wy_recv, head, plane, j, False)
-
-    each(HEADS, sent_wide)
+    basis_copy.wait()
     for j in range(2):
-        z_send(wide_sum, wide_z, wz_send, wz_recv, j, False)
-
-        @pl.when(owner_z(j) != z)
-        def _():
-            stat_z_copy(j, z).wait_send()
-
-        others(PLANES, y, lambda plane: stat_pass(j, plane).wait_send())
         relay_basis(j, True, False)
-
-    @pl.when(owns)
-    def _():
-        others(RING, z, lambda d: stat_share(d).wait_send())
-        share_basis(True, False)
+    pl.when(owns)(lambda: share_basis(True, False))
 
 
 def body(queries, keys, omega, block_offsets):
@@ -841,13 +859,13 @@
             jax.ShapeDtypeStruct((HEADS * RANK, KEYS), F32),
         ),
         in_specs=[
-            pl.BlockSpec(memory_space=pltpu.SMEM),
-            pl.BlockSpec(memory_space=pltpu.VMEM),
+            pl.BlockSpec(memory_space=pl.ANY),
+            pl.BlockSpec(memory_space=pl.ANY),
             pl.BlockSpec(memory_space=pl.ANY),
             pl.BlockSpec(memory_space=pl.ANY),
         ],
         out_specs=(
-            pl.BlockSpec(memory_space=pltpu.VMEM),
+            pl.BlockSpec(memory_space=pl.ANY),
             pl.BlockSpec(memory_space=pl.ANY),
         ),
         scratch_shapes=[
@@ -880,7 +898,10 @@
             vmem((RING, *panel), BF16),
             vmem((HEADS, *panel), BF16),
             vmem((HEADS * RANK, KEYS), F32),
-            dma(2),
+            vmem((16, HEADS * RANK), F32),
+            pltpu.SMEM((4,), jnp.int32),
+            vmem((2, KVH * HEADS * HEAD), BF16),
+            dma(4),
             dma(HEADS),
             dma(KVH), dma(KVH),
             dma(KVH), dma(KVH),

time: 128 us -> 126 us (0.984)
  Pallas kernels: 120 us -> 118 us
    pallas_call x1, Pallas kernels: 120 us -> 118 us  [body(): pl.pallas_call(kernel, out_shape=(jax.ShapeDtypeStruct((16, HEADS * RANK)...]
where the time goes in v5:
time: 126 us; the launch traced here: 123 us
  Pallas kernels  118 us (94%)
  other arithmetic  4.67 us (4%)
    pallas_call x1, Pallas kernels, body(): pl.pallas_call(kernel, out_shape=(jax.ShapeDtypeStruct((16, HEADS * RANK)...  118 us
    mul x2, other arithmetic, body(): return (basis * math.sqrt(QUERIES), projection * math.sqrt(SEQ * KEYS))  4.67 us

profile of v5, /device:TPU:24, one launch (start us, length us, event | category | flops | bytes accessed | tf_op | source)
XLA Modules:
  0.0 123.2 jit_solution(2672569812498609220)
XLA Ops:
  0.6 117.9 %range_finder.1 = (f32[16,512]{1,0:T(8,128)}, f32[512,1024]{1,0:T(8,128)}) custom-call(s32[4]{0:T(128)} %offsets_hbm.1, bf16[2,8192]{1,0:T(2,128)(2,1)} %q_hbm.1, bf16[128,1024]{1,0:T(8,128)(2,1)} %k_hbm.1, bf16[1024,512]{1,0:T(8,128)(2,1)} %omega_hbm.1), custom_call_target="tpu_custom_call" | custom-call | flops 6000000000 | bytes 8388608 | tf_op jit(solution)/shard_map/range_finder/pallas_call | solution.py:855
  118.5 1.4 %broadcast_multiply_fusion.1 = f32[16,512]{1,0:T(8,128)} fusion(f32[16,512]{1,0:T(8,128)} %get-tuple-element.4), kind=kLoop, calls=%fused_computation.1 | loop fusion | flops 8192 | bytes 65536 | tf_op jit(solution)/shard_map/mul | solution.py:926
  119.9 3.3 %broadcast_multiply_fusion = f32[512,1024]{1,0:T(8,128)} fusion(f32[512,1024]{1,0:T(8,128)} %get-tuple-element.5), kind=kLoop, calls=%fused_computation | loop fusion | flops 524288 | bytes 4194304 | tf_op jit(solution)/shard_map/mul | solution.py:926

commit v6 on v5

--- a/solution.py
+++ b/solution.py
@@ -846,6 +846,29 @@
     for j in range(2):
         relay_basis(j, True, False)
     pl.when(owns)(lambda: share_basis(True, False))
+
+
+def scale_kernel(basis_ref, rows_ref, basis_out, rows_out):
+    basis_out[...] = basis_ref[...] * math.sqrt(QUERIES)
+    rows_out[...] = rows_ref[...] * math.sqrt(SEQ * KEYS)
+
+
+def scaled(basis, projection):
+    steps = 2
+    rows = projection.shape[0] // steps
+    whole = pl.BlockSpec(basis.shape, lambda i: (0, 0))
+    part = pl.BlockSpec((rows, projection.shape[1]), lambda i: (i, 0))
+    return pl.pallas_call(
+        scale_kernel,
+        out_shape=(
+            jax.ShapeDtypeStruct(basis.shape, F32),
+            jax.ShapeDtypeStruct(projection.shape, F32),
+        ),
+        grid=(steps,),
+        in_specs=[whole, part],
+        out_specs=(whole, part),
+        name="scale_results",
+    )(basis, projection)
 
 
 def body(queries, keys, omega, block_offsets):
@@ -923,7 +946,7 @@
         ),
         name="range_finder",
     )(block_offsets, queries, keys, omega)
-    return basis * math.sqrt(QUERIES), projection * math.sqrt(SEQ * KEYS)
+    return scaled(basis, projection)
 
 
 def solution(mesh):

time: 126 us -> 123 us (0.976)
  other arithmetic: 4.67 us -> 0 us
  Pallas kernels: 118 us -> 121 us
    mul x2 -> x0, other arithmetic: 4.67 us -> none  [body(): return (basis * math.sqrt(QUERIES), projection * math.sqrt(SEQ * KEYS))]
    pallas_call x0 -> x1, Pallas kernels: none -> 2.66 us  [scaled(): pl.pallas_call(scale_kernel, out_shape=(jax.ShapeDtypeStruct(basis.shape,...]
where the time goes in v6:
time: 123 us; the launch traced here: 121 us
  Pallas kernels  121 us (98%)
    pallas_call x1, Pallas kernels, body(): pl.pallas_call(kernel, out_shape=(jax.ShapeDtypeStruct((16, HEADS * RANK)...  118 us
    pallas_call x1, Pallas kernels, scaled(): pl.pallas_call(scale_kernel, out_shape=(jax.ShapeDtypeStruct(basis.shape,...  2.66 us

profile of v6, /device:TPU:24, one launch (start us, length us, event | category | flops | bytes accessed | tf_op | source)
XLA Modules:
  0.0 121.2 jit_solution(13000408685231508144)
XLA Ops:
  0.6 117.9 %range_finder.1 = (f32[16,512]{1,0:T(8,128)}, f32[512,1024]{1,0:T(8,128)}) custom-call(s32[4]{0:T(128)} %offsets_hbm.1, bf16[2,8192]{1,0:T(2,128)(2,1)} %q_hbm.1, bf16[128,1024]{1,0:T(8,128)(2,1)} %k_hbm.1, bf16[1024,512]{1,0:T(8,128)(2,1)} %omega_hbm.1), custom_call_target="tpu_custom_call" | custom-call | flops 6000000000 | bytes 8388608 | tf_op jit(solution)/shard_map/range_finder/pallas_call | solution.py:878
  118.5 2.7 %scale_results.1 = (f32[16,512]{1,0:T(8,128)}, f32[512,1024]{1,0:T(8,128)}) custom-call(f32[16,512]{1,0:T(8,128)} %get-tuple-element.4.basis_ref, f32[512,1024]{1,0:T(8,128)} %get-tuple-element.5.rows_ref), custom_call_target="tpu_custom_call" | custom-call | tf_op jit(solution)/shard_map/scale_results/pallas_call | solution.py:861

commit v7 on v6

--- a/solution.py
+++ b/solution.py
@@ -854,7 +854,7 @@
 
 
 def scaled(basis, projection):
-    steps = 2
+    steps = 1
     rows = projection.shape[0] // steps
     whole = pl.BlockSpec(basis.shape, lambda i: (0, 0))
     part = pl.BlockSpec((rows, projection.shape[1]), lambda i: (i, 0))

time: 123 us -> 124 us (level)
  no operation moved by 1% of the time
where the time goes in v7:
time: 124 us; the launch traced here: 122 us
  Pallas kernels  121 us (98%)
    pallas_call x1, Pallas kernels, body(): pl.pallas_call(kernel, out_shape=(jax.ShapeDtypeStruct((16, HEADS * RANK)...  118 us
    pallas_call x1, Pallas kernels, scaled(): pl.pallas_call(scale_kernel, out_shape=(jax.ShapeDtypeStruct(basis.shape,...  3.12 us

profile of v7, /device:TPU:24, one launch (start us, length us, event | category | flops | bytes accessed | tf_op | source)
XLA Modules:
  0.0 121.7 jit_solution(15394465897233513383)
XLA Ops:
  0.6 117.9 %range_finder.1 = (f32[16,512]{1,0:T(8,128)}, f32[512,1024]{1,0:T(8,128)}) custom-call(s32[4]{0:T(128)} %offsets_hbm.1, bf16[2,8192]{1,0:T(2,128)(2,1)} %q_hbm.1, bf16[128,1024]{1,0:T(8,128)(2,1)} %k_hbm.1, bf16[1024,512]{1,0:T(8,128)(2,1)} %omega_hbm.1), custom_call_target="tpu_custom_call" | custom-call | flops 6000000000 | bytes 8388608 | tf_op jit(solution)/shard_map/range_finder/pallas_call | solution.py:878
  118.5 3.1 %scale_results.1 = (f32[16,512]{1,0:T(8,128)}, f32[512,1024]{1,0:T(8,128)}) custom-call(f32[16,512]{1,0:T(8,128)} %get-tuple-element.4.basis_ref, f32[512,1024]{1,0:T(8,128)} %get-tuple-element.5.rows_ref), custom_call_target="tpu_custom_call" | custom-call | tf_op jit(solution)/shard_map/scale_results/pallas_call | solution.py:861
